TPU v7x, 256 devices: a whole 4x4x8 slice. The times are simulated.
256 devices in a mesh: cache: 32 (over y, z), head: 8 (over x, core).
Axes of the slice: x: 4, y: 4, z: 8, core: 2. Of those that a mesh axis runs over, the one named last changes fastest.
Arguments:
- candidates: bfloat16 [65536, 1024], P(('cache', 'head')), may hold values from -6 to 6
- proj_in: bfloat16 [2, 1024, 4096], P(None, None, 'head'), may hold values from -0.1875 to 0.1875
- proj_out: bfloat16 [2, 1024, 1024], P(None, 'head'), may hold values from -0.1875 to 0.1875
- page_pool: bfloat16 [32, 32, 2, 2, 128, 2048], P('cache', None, None, None, None, 'head'), may hold values from -6 to 6
- page_owner: int32 [64, 16, 1], P('cache'), may hold values from 0 to 31; in each aligned block of 32 rows (0 to 31, 32 to 63, ..., all dimensions but the last counted through in order) at most 2 rows name the same one
- history_pages: int32 [64], P('cache'), may hold values from 9 to 16, as said below
Outputs:
- scored: bfloat16 [65536, 1024], P(('cache', 'head'))
Inputs may be any that keep to these rules, and one draw needn't show every extreme that they name: `page_owner`: in the pages of the users of one scoring group no owner is named more than 2 times, a bound that some block reaches. `history_pages`: some user has all 16 pages live.
All inputs are finite; a program needn't handle non-finite values.
Results may differ from a plain program's by a relative error of at most 0.02.
Values may be sent and summed in bfloat16 or wider, within the bound.
A program may use at most 128 MiB of HBM per device.

v0:
```python
import jax
import jax.numpy as jnp
from jax import lax
from jax.sharding import PartitionSpec as P

DH = 128


def hstu_layer(state, w_in, w_out, history, live, denom, users_here, cand, heads_local):
    xf = state.astype(jnp.float32)
    normed = (xf * lax.rsqrt(jnp.mean(xf * xf, axis=-1, keepdims=True) + 1e-06)).astype(
        jnp.bfloat16
    )
    act = jax.nn.silu(
        jnp.dot(
            lax.all_gather(normed, "head", axis=0, tiled=True),
            w_in,
            preferred_element_type=jnp.float32,
        )
    ).astype(jnp.bfloat16)
    group_rows = act.shape[0]
    act = act.reshape(users_here, cand, heads_local, 4, DH)
    gate = act[:, :, :, 0, :]
    value = act[:, :, :, 1, :]
    query = act[:, :, :, 2, :]
    key = act[:, :, :, 3, :]
    hist_key = history[:, :, :, 0, :]
    hist_value = history[:, :, :, 1, :]
    scale = DH ** (-0.5)
    scores = (
        jnp.einsum("uchd,uehd->uhce", query, hist_key, preferred_element_type=jnp.float32) * scale
    )
    weights = (
        jnp.where(live[:, None, None, :], jax.nn.silu(scores), 0.0) / denom[:, None, None, None]
    )
    weights = weights.astype(jnp.bfloat16)
    own = jnp.sum(query.astype(jnp.float32) * key.astype(jnp.float32), axis=-1) * scale
    own_weight = (jax.nn.silu(own) / denom[:, None, None]).astype(jnp.bfloat16)
    attended = jnp.einsum(
        "uhce,uehd->uchd", weights, hist_value, preferred_element_type=jnp.float32
    )
    attended = attended + own_weight.astype(jnp.float32)[..., None] * value.astype(jnp.float32)
    attended = attended.reshape(group_rows, heads_local * DH)
    first, second = lax.psum(
        (jnp.sum(attended, axis=-1), jnp.sum(attended * attended, axis=-1)), "head"
    )
    full_width = heads_local * DH * lax.axis_size("head")
    mean_row = (first / full_width)[:, None]
    square_row = (second / full_width)[:, None]
    gated = (
        (attended - mean_row)
        * lax.rsqrt(square_row - mean_row * mean_row + 1e-05)
        * gate.reshape(group_rows, heads_local * DH).astype(jnp.float32)
    ).astype(jnp.bfloat16)
    update = lax.psum_scatter(
        jnp.dot(gated, w_out, preferred_element_type=jnp.float32).astype(jnp.bfloat16),
        "head",
        scatter_dimension=0,
        tiled=True,
    ).astype(jnp.float32)
    return (xf + update).astype(jnp.bfloat16)


def shards(candidates, proj_in, proj_out, page_pool, page_owner, history_pages):
    heads_local = proj_out.shape[1] // DH
    users_here = page_owner.shape[0]
    pages_user = page_owner.shape[1]
    group_rows = candidates.shape[0] * lax.axis_size("head")
    cand = group_rows // users_here
    layers = proj_in.shape[0]
    pool_local = page_pool[0]
    slot_cap = pool_local.shape[1]
    page_len = pool_local.shape[3]
    width = pool_local.shape[4]
    owners = page_owner[:, :, 0].reshape(-1)
    page_count = owners.shape[0]
    order = jnp.arange(page_count)
    earlier = (owners[:, None] == owners[None, :]) & (order[None, :] < order[:, None])
    slots = jnp.sum(earlier.astype(jnp.int32), axis=1)
    source_rows = owners * slot_cap + slots
    events = pages_user * page_len
    live = jnp.arange(events)[None, :] < (history_pages * page_len)[:, None]
    denom = (history_pages * page_len + 1).astype(jnp.float32)
    arrived = lax.all_to_all(pool_local, "cache", split_axis=0, concat_axis=0, tiled=True)
    state = candidates
    for layer in range(layers):
        received = arrived[:, :, layer]
        picked = received.reshape(-1, page_len, width)[source_rows]
        history = picked.reshape(users_here, events, heads_local, 2, DH)
        state = hstu_layer(
            state,
            proj_in[layer],
            proj_out[layer],
            history,
            live,
            denom,
            users_here,
            cand,
            heads_local,
        )
    return state


def solution(mesh):
    return jax.shard_map(
        shards,
        mesh=mesh,
        in_specs=(
            P(("cache", "head"), None),
            P(None, None, "head"),
            P(None, "head", None),
            P("cache", None, None, None, None, "head"),
            P("cache", None, None),
            P("cache"),
        ),
        out_specs=P(("cache", "head"), None),
        check_vma=False,
    )
```

profile of v0, /device:TPU:7, one launch (start us, length us, event | category | flops | bytes accessed | tf_op | source)
XLA Modules:
  0.0 454.8 jit_solution(13030836878641582231)
XLA Ops:
  6.5 11.6 %all-to-all-start = ((bf16[32,2,2,128,256]{4,3,2,1,0:T(8,128)(2,1)}), bf16[32,2,2,128,256]{4,3,2,1,0:T(8,128)(2,1)}, u32[]{:S(2)}, u32[]{:S(2)}) async-start(bf16[32,2,2,128,256]{4,3,2,1,0:T(8,128)(2,1)} %bitcast.106), calls=%async_computation | async-start | bytes 16777216 | tf_op jit(solution)/shard_map/all_to_all | solution.py:84
  21.1 34.4 %all-gather.3.cloned.1.call-done = bf16[2048,1024]{1,0:T(8,128)(2,1)} async-done(((bf16[256,1024]{1,0:T(8,128)(2,1)}), bf16[2048,1024]{1,0:T(8,128)(2,1)}) %all-gather.3.cloned.1.call-update) | async-done | bytes 4194320 | tf_op jit(solution)/shard_map/all_gather | solution.py:16
  55.5 6.5 %multiply_convert_fusion.1 = bf16[2048,512]{1,0:T(8,128)(2,1)} fusion(bf16[2048,1024]{1,0:T(8,128)(2,1)} %all-gather.3.cloned.1.call-done, bf16[2,1024,512]{2,1,0:T(8,128)(2,1)S(1)} %copy-done.5), kind=kOutput, calls=%fused_computation.9 | convolution fusion | flops 2152726528 | bytes 7340032 | tf_op jit(solution)/shard_map/dot_general | solution.py:15
  64.6 4.5 fusion.61
  71.4 3.5 copy.49
  76.9 129.5 %all-to-all-done = bf16[32,2,2,128,256]{4,3,2,1,0:T(8,128)(2,1)} async-done(((bf16[32,2,2,128,256]{4,3,2,1,0:T(8,128)(2,1)}), bf16[32,2,2,128,256]{4,3,2,1,0:T(8,128)(2,1)}, u32[]{:S(2)}, u32[]{:S(2)}) %all-to-all-start) | async-done | bytes 8388640 | tf_op jit(solution)/shard_map/all_to_all | solution.py:84
  206.4 6.0 %fusion.59 = (bf16[32,2,1,128,256]{4,3,2,1,0:T(8,128)(2,1)}, bf16[32,2,1,128,256]{4,3,2,1,0:T(8,128)(2,1)}) fusion(bf16[32,2,2,128,256]{4,3,2,1,0:T(8,128)(2,1)} %all-to-all-done), kind=kLoop, calls=%fused_computation.94 | loop fusion | bytes 16777216 | tf_op jit(solution)/shard_map/slice | solution.py:87
  212.3 4.2 gather_fusion
  219.1 4.2 fusion.62
  223.3 4.6 %copy.45 = bf16[2,2048,1,1,128]{1,4,0,3,2:T(8,128)(2,1)S(1)} copy(bf16[2,2048,1,1,128]{4,3,1,0,2:T(2,128)(2,1)} %get-tuple-element.25) | data formatting | bytes 2097152
  227.9 10.2 %fusion.57 = (f32[2,1024]{1,0:T(2,128)S(1)}, f32[2,1024]{1,0:T(2,128)S(1)}, f32[2,1024,1,128]{1,3,0,2:T(8,128)S(1)}) fusion(bf16[2,1024,1,1,128]{1,4,0,3,2:T(8,128)(2,1)} %copy.49, f32[2,1024]{1,0:T(2,128)S(1)} %fusion.48, f32[2]{0:T(128)S(1)} %get-tuple-element.34, pred[2,2048]{1,0:T(4,128)(4,1)S(1)} %iota_compare_fusion, ...), kind=kOutput, calls=%fused_computation.92 | convolution fusion | flops 2182606848 | bytes 4222984 | tf_op jit(solution)/shard_map/uhce,uehd->uchd/dot_general | solution.py:39
  238.1 22.9 %all-reduce.1 = (f32[2048]{0:T(1024)S(1)}, f32[2048]{0:T(1024)S(1)}) all-reduce(f32[2048]{0:T(1024)S(1)} %get-tuple-element.37, f32[2048]{0:T(1024)S(1)} %get-tuple-element.38), channel_id=1, replica_groups=mesh['cache'=32,'head'=8] {'head'}, use_global_device_ids=true, to_apply=%region_6.7 | all-reduce | flops 4096 | bytes 32768 | tf_op jit(solution)/shard_map/psum | solution.py:44
  261.5 4.1 convolution_convert_fusion.1
  265.7 44.8 %reduce-scatter.3.cloned.1.call-done = bf16[256,1024]{1,0:T(8,128)(2,1)} async-done(((bf16[2048,1024]{1,0:T(8,128)(2,1)}), bf16[256,1024]{1,0:T(8,128)(2,1)}) %reduce-scatter.3.cloned.1.call-update) | async-done | bytes 524304 | tf_op jit(solution)/shard_map/reduce_scatter | solution.py:55
  313.8 4.2 gather_fusion.1
  320.6 4.3 fusion.63
  324.8 5.9 %copy.51 = bf16[2,2048,1,1,128]{1,4,0,3,2:T(8,128)(2,1)} copy(bf16[2,2048,1,1,128]{4,3,1,0,2:T(2,128)(2,1)} %get-tuple-element.27) | data formatting | bytes 2097152
  330.7 17.0 %all-gather.5.cloned.1.call-done = bf16[2048,1024]{1,0:T(8,128)(2,1)} async-done(((bf16[256,1024]{1,0:T(8,128)(2,1)}), bf16[2048,1024]{1,0:T(8,128)(2,1)}) %all-gather.5.cloned.1.call-update) | async-done | bytes 4194320 | tf_op jit(solution)/shard_map/all_gather | solution.py:16
  347.7 6.8 %multiply_convert_fusion = bf16[2048,512]{1,0:T(8,128)(2,1)} fusion(bf16[2048,1024]{1,0:T(8,128)(2,1)} %all-gather.5.cloned.1.call-done, bf16[2,1024,512]{2,1,0:T(8,128)(2,1)} %param.7), kind=kOutput, calls=%fused_computation.8 | convolution fusion | flops 2152726528 | bytes 7340032 | tf_op jit(solution)/shard_map/dot_general | solution.py:15
  357.0 4.5 fusion.60
  367.8 10.2 %fusion.56 = (f32[2,1024]{1,0:T(2,128)S(1)}, f32[2,1024]{1,0:T(2,128)S(1)}, f32[2,1024,1,128]{1,3,0,2:T(8,128)S(1)}) fusion(bf16[2,1024,1,1,128]{1,4,0,3,2:T(8,128)(2,1)} %copy.55, f32[2,1024]{1,0:T(2,128)S(1)} %fusion.47, f32[2]{0:T(128)S(1)} %get-tuple-element.34, pred[2,2048]{1,0:T(4,128)(4,1)S(1)} %iota_compare_fusion, ...), kind=kOutput, calls=%fused_computation.91 | convolution fusion | flops 2182606848 | bytes 4222984 | tf_op jit(solution)/shard_map/uhce,uehd->uchd/dot_general | solution.py:39
  378.0 22.9 %all-reduce = (f32[2048]{0:T(1024)S(1)}, f32[2048]{0:T(1024)S(1)}) all-reduce(f32[2048]{0:T(1024)S(1)} %bitcast.110, f32[2048]{0:T(1024)S(1)} %bitcast.109), channel_id=1, replica_groups=mesh['cache'=32,'head'=8] {'head'}, use_global_device_ids=true, to_apply=%region_13.14 | all-reduce | flops 4096 | bytes 32768 | tf_op jit(solution)/shard_map/psum | solution.py:44
  401.4 4.1 convolution_convert_fusion
  405.6 40.6 %reduce-scatter.5.cloned.1.call-done = bf16[256,1024]{1,0:T(8,128)(2,1)} async-done(((bf16[2048,1024]{1,0:T(8,128)(2,1)}), bf16[256,1024]{1,0:T(8,128)(2,1)}) %reduce-scatter.5.cloned.1.call-update) | async-done | bytes 524304 | tf_op jit(solution)/shard_map/reduce_scatter | solution.py:55
  (62 shorter events, 30.1 us)
Async XLA Ops:
  6.5 11.7 %copy-start = (bf16[256,1024]{1,0:T(8,128)(2,1)S(1)}, bf16[256,1024]{1,0:T(8,128)(2,1)}, u32[]{:S(2)}) copy-start(bf16[256,1024]{1,0:T(8,128)(2,1)} %param.6) | copy-start | bytes 1572868
  6.5 13.4 %copy-start.4 = (s32[2,16,1]{1,2,0:T(1,128)S(1)}, s32[2,16,1]{1,2,0:T(1,128)}, u32[]{:S(2)}) copy-start(s32[2,16,1]{1,2,0:T(1,128)} %param.10) | copy-start | bytes 388
  6.5 14.4 %copy-start.6 = (s32[2]{0:T(128)S(1)}, s32[2]{0:T(128)}, u32[]{:S(2)}) copy-start(s32[2]{0:T(128)} %param.11) | copy-start | bytes 28
  6.5 49.0 %copy-start.5 = (bf16[2,1024,512]{2,1,0:T(8,128)(2,1)S(1)}, bf16[2,1024,512]{2,1,0:T(8,128)(2,1)}, u32[]{:S(2)}) copy-start(bf16[2,1024,512]{2,1,0:T(8,128)(2,1)} %param.7) | copy-start | bytes 6291460
  6.5 199.8 %all-to-all-start = ((bf16[32,2,2,128,256]{4,3,2,1,0:T(8,128)(2,1)}), bf16[32,2,2,128,256]{4,3,2,1,0:T(8,128)(2,1)}, u32[]{:S(2)}, u32[]{:S(2)}) async-start(bf16[32,2,2,128,256]{4,3,2,1,0:T(8,128)(2,1)} %bitcast.106), calls=%async_computation | async-start | bytes 16777216 | tf_op jit(solution)/shard_map/all_to_all | solution.py:84
  18.1 37.4 %all-gather.3.cloned.1.call-start = ((), (), s32[]{:S(2)}) async-start(), calls=%async_computation.3 | async-start | bytes 4718592 | tf_op jit(solution)/shard_map/all_gather | solution.py:16
  19.4 291.1 %reduce-scatter.3.cloned.1.call-start = ((), (), s32[]{:S(2)}) async-start(), calls=%async_computation.4 | async-start | bytes 4718592 | tf_op jit(solution)/shard_map/reduce_scatter | solution.py:55
  265.6 82.1 %all-gather.5.cloned.1.call-start = ((), (), s32[]{:S(2)}) async-start(), calls=%async_computation.5 | async-start | bytes 4718592 | tf_op jit(solution)/shard_map/all_gather | solution.py:16
  313.8 132.4 %reduce-scatter.5.cloned.1.call-start = ((), (), s32[]{:S(2)}) async-start(), calls=%async_computation.6 | async-start | bytes 4718592 | tf_op jit(solution)/shard_map/reduce_scatter | solution.py:55
  361.5 4.5 copy-start.3
  361.5 6.3 %copy-start.2 = (bf16[2,1024,1,1,128]{4,3,1,0,2:T(2,128)(2,1)S(1)}, bf16[2,1024,1,1,128]{4,3,1,0,2:T(2,128)(2,1)}, u32[]{:S(2)}) copy-start(bf16[2,1024,1,1,128]{4,3,1,0,2:T(2,128)(2,1)} %get-tuple-element.19) | copy-start | bytes 1572868
  405.6 40.6 %copy-start.1 = (bf16[256,1024]{1,0:T(8,128)(2,1)S(1)}, bf16[256,1024]{1,0:T(8,128)(2,1)}, u32[]{:S(2)}) copy-start(bf16[256,1024]{1,0:T(8,128)(2,1)} %reduce-scatter.3.cloned.1.call-done) | copy-start | bytes 1572868
Sparse Core Ops, SparseCore 0:
  20.8 34.6 all-gather.2
  265.8 44.6 reduce-scatter.2
  313.9 33.7 all-gather.4
  405.7 40.4 reduce-scatter.4
where the time goes:
time: 457 us; the launch traced here: 455 us
  waiting for transfers between devices  266 us (58%)
  local copies, waits for them, and re-layouts  64 us (14%)
  blocking collectives  45.8 us (10%)
  matrix products  41.9 us (9%)
  between operations  13.3 us (3%)
  starting transfers between devices  11.8 us (3%)
  other arithmetic  11.8 us (3%)
    all_to_all x1, waiting for transfers between devices, shards(): lax.all_to_all(pool_local, 'cache', split_axis=0, concat_axis=0, tiled=True)  129 us
    reduce_scatter x2, waiting for transfers between devices, hstu_layer(): lax.psum_scatter(jnp.dot(gated, w_out, preferred_element_type=jnp.float32...  85.4 us
    all_gather x2, waiting for transfers between devices, hstu_layer(): lax.all_gather(normed, 'head', axis=0, tiled=True)  51.4 us
    psum x2, blocking collectives, hstu_layer(): lax.psum((jnp.sum(attended, axis=-1), jnp.sum(attended * attended, axis=-...  45.8 us
    unnamed x23, local copies, waits for them, and re-layouts  21.2 us
    dot_general x2, matrix products, hstu_layer(): jnp.einsum('uhce,uehd->uchd', weights, hist_value, preferred_element_type...  20.4 us
    dot_general x2, matrix products, hstu_layer(): jnp.dot(lax.all_gather(normed, 'head', axis=0, tiled=True), w_in, preferr...  13.3 us
    all_to_all x1, starting transfers between devices, shards(): lax.all_to_all(pool_local, 'cache', split_axis=0, concat_axis=0, tiled=True)  11.6 us
  transfers between devices with their start and end apart: 5, of which 5 were waited for; matrix products, arithmetic and copies ran while one was open for 9% of the time, Pallas kernels for 0%

commit v1 on v0

v1 whole, which is shorter than its diff:
```python
import jax
import jax.numpy as jnp
from jax import lax
from jax.experimental import pallas as pl
from jax.experimental.pallas import tpu as pltpu
from jax.sharding import PartitionSpec as P

MESH = pl.DeviceIdType.MESH
DH = 128
D = 1024
PAGE = 128
LAYERS = 2
USERS = 2
PAGES = 16
NY = 4
NZ = 8
NX = 4
HEADS = 8
BLOCK = 256
C = 8
ZERO = NZ * C
REQ = 16
OFFSETS = (4, 3, 5, 2, 6, 1, 7, 0)
F32 = jnp.float32
BF16 = jnp.bfloat16


def half_silu(t):
    return t * jnp.tanh(t) + t


def kernel(
    src,
    recip,
    cand,
    w_in,
    w_out,
    req_out,
    pool,
    out,
    *scratch,
):
    (
        arr,
        pack,
        rows_all,
        w_all,
        gate_send,
        gate_recv,
        att_send,
        att_recv,
    ) = [scratch[2 * i : 2 * i + 2] for i in range(8)]
    ybuf = scratch[16:32]
    (
        q_buf,
        k_buf,
        v_buf,
        acc,
        state,
        req_in,
        req_smem,
        y_ssem,
        y_rsem,
        z_ssem,
        z_rsem,
        req_ssem,
        req_rsem,
        smem_sem,
        row_ssem,
        row_fsem,
        row_rsem,
        w_ssem,
        w_fsem,
        w_rsem,
        gate_ssem,
        gate_rsem,
        att_ssem,
        att_rsem,
    ) = scratch[32:]

    me_c = lax.axis_index("cache")
    me_h = lax.axis_index("head")
    my_y = me_c // NZ
    my_z = lax.rem(me_c, NZ)
    my_x = me_h // 2
    core = lax.rem(me_h, 2)
    sibling = my_x * 2 + (1 - core)

    def y_peer(dy):
        return lax.rem(my_y + dy, NY)

    def z_peer(dz):
        return lax.rem(my_z + dz, NZ)

    def head_peer(dx, dcore):
        return lax.rem(my_x + dx, NX) * 2 + lax.rem(core + dcore, 2)

    head_steps = [(dx, dc) for dx in range(NX) for dc in range(2) if (dx, dc) != (0, 0)]

    barrier = pltpu.get_barrier_semaphore()
    for dy in range(1, NY):
        pl.semaphore_signal(
            barrier, inc=1, device_id=(y_peer(dy) * NZ + my_z, me_h), device_id_type=MESH
        )
    for dz in range(1, NZ):
        pl.semaphore_signal(
            barrier, inc=1, device_id=(my_y * NZ + z_peer(dz), me_h), device_id_type=MESH
        )
    for dx, dc in head_steps:
        pl.semaphore_signal(
            barrier, inc=1, device_id=(me_c, head_peer(dx, dc)), device_id_type=MESH
        )

    def remote(src_ref, dst_ref, send, recv, cache, head):
        return pltpu.make_async_remote_copy(
            src_ref=src_ref,
            dst_ref=dst_ref,
            send_sem=send,
            recv_sem=recv,
            device_id=(cache, head),
            device_id_type=MESH,
        )

    def y_copy(layer, i, dy):
        group = y_peer(dy) * NZ + z_peer(OFFSETS[i])
        return remote(
            pool.at[group, :, layer],
            ybuf[layer * NZ + i].at[pl.ds(my_y * 2, 2)],
            y_ssem.at[layer, i, dy],
            y_rsem.at[layer, i, my_y],
            y_peer(dy) * NZ + my_z,
            me_h,
        )

    def y_local(layer, i):
        group = my_y * NZ + z_peer(OFFSETS[i])
        return pltpu.make_async_copy(
            pool.at[group, :, layer],
            ybuf[layer * NZ + i].at[pl.ds(my_y * 2, 2)],
            y_rsem.at[layer, i, my_y],
        )

    def y_start(layer, i):
        for dy in (2, 1, 3):
            y_copy(layer, i, dy).start()
        y_local(layer, i).start()

    def y_wait(layer, i):
        for dy in range(1, NY):
            other = y_peer(dy)
            place = ybuf[layer * NZ + i].at[pl.ds(other * 2, 2)]
            remote(
                place,
                place,
                y_ssem.at[layer, i, dy],
                y_rsem.at[layer, i, other],
                other * NZ + my_z,
                me_h,
            ).wait_recv()
        y_local(layer, i).wait()

    def z_copy(layer, i):
        column = z_peer(OFFSETS[i])
        return remote(
            pack[layer].at[i],
            arr[layer].at[pl.ds(my_z * C, C)],
            z_ssem.at[layer, i],
            z_rsem.at[layer, my_z],
            my_y * NZ + column,
            me_h,
        )

    def z_wait(layer, dz):
        column = z_peer(dz)
        place = arr[layer].at[pl.ds(column * C, C)]
        remote(
            place,
            place,
            z_ssem.at[layer, 0],
            z_rsem.at[layer, column],
            my_y * NZ + column,
            me_h,
        ).wait_recv()

    def pack_send(layer, i):
        y_wait(layer, i)
        column = z_peer(OFFSETS[i])
        buf = ybuf[layer * NZ + i]
        for j in range(C):
            page = buf[req_smem[column, 0, j]]
            if OFFSETS[i] == 0:
                arr[layer][my_z * C + j] = page
            else:
                pack[layer][i, j] = page
        if OFFSETS[i] != 0:
            z_copy(layer, i).start()

    def rows_start(layer):
        place = rows_all[layer].at[me_h]
        for dx in (2, 1, 3):
            remote(
                place,
                place,
                row_ssem.at[layer, dx],
                row_rsem.at[layer, me_h],
                me_c,
                head_peer(dx, 0),
            ).start()
        remote(
            place, place, row_ssem.at[layer, 0], row_rsem.at[layer, me_h], me_c, sibling
        ).start()

    def rows_wait(layer):
        for dx in (1, 3, 2):
            source = head_peer(dx, 0)
            place = rows_all[layer].at[source]
            copy = remote(
                place, place, row_fsem.at[layer, dx], row_rsem.at[layer, source], me_c, sibling
            )
            copy.wait_recv()
            copy.start()
        for dx in (0, 1, 3, 2):
            source = head_peer(dx, 1)
            place = rows_all[layer].at[source]
            remote(
                place, place, row_fsem.at[layer, dx], row_rsem.at[layer, source], me_c, sibling
            ).wait_recv()

    def rows_drain(layer):
        place = rows_all[layer].at[me_h]
        for dx in range(NX):
            remote(
                place, place, row_ssem.at[layer, dx], row_rsem.at[layer, me_h], me_c, sibling
            ).wait_send()
        for dx in range(1, NX):
            remote(
                place, place, row_fsem.at[layer, dx], row_rsem.at[layer, me_h], me_c, sibling
            ).wait_send()

    def w_place(layer, source):
        return w_all[layer].at[source]

    def w_start():
        for layer in range(LAYERS):
            for dx in (2, 1, 3):
                remote(
                    w_out.at[layer],
                    w_place(layer, me_h),
                    w_ssem.at[layer, dx],
                    w_rsem.at[layer, me_h],
                    me_c,
                    head_peer(dx, 0),
                ).start()
            remote(
                w_out.at[layer],
                w_place(layer, me_h),
                w_ssem.at[layer, 0],
                w_rsem.at[layer, me_h],
                me_c,
                sibling,
            ).start()
            w_all[layer][me_h] = w_out[layer]

    def w_forward(layer):
        for dx in (1, 3, 2):
            source = head_peer(dx, 0)
            place = w_place(layer, source)
            copy = remote(
                place, place, w_fsem.at[layer, dx], w_rsem.at[layer, source], me_c, sibling
            )
            copy.wait_recv()
            copy.start()

    def w_wait(layer):
        for dx in range(NX):
            source = head_peer(dx, 1)
            place = w_place(layer, source)
            remote(
                place, place, w_fsem.at[layer, dx], w_rsem.at[layer, source], me_c, sibling
            ).wait_recv()

    def w_drain(layer):
        place = w_place(layer, me_h)
        for dx in range(NX):
            remote(
                place, place, w_ssem.at[layer, dx], w_rsem.at[layer, me_h], me_c, sibling
            ).wait_send()
        for dx in range(1, NX):
            remote(
                place, place, w_fsem.at[layer, dx], w_rsem.at[layer, me_h], me_c, sibling
            ).wait_send()

    def norm_rows(layer):
        xf = state[...]
        normed = xf * lax.rsqrt(jnp.mean(xf * xf, axis=-1, keepdims=True) + 1e-06)
        rows_all[layer][me_h] = normed.astype(BF16)

    def project(layer):
        def body(i, carry):
            act = jnp.dot(rows_all[layer][i], w_in[layer], preferred_element_type=F32)
            act = half_silu(act * 0.5).astype(BF16)
            gate_send[layer][i] = act[:, :DH]
            v_buf[i] = act[:, DH : 2 * DH]
            q_buf[i] = act[:, 2 * DH : 3 * DH]
            k_buf[i] = act[:, 3 * DH :]
            return carry

        lax.fori_loop(0, HEADS, body, 0)

    def gate_copy(layer, dx, dc, index):
        peer = head_peer(dx, dc)
        return remote(
            gate_send[layer].at[peer],
            gate_recv[layer].at[me_h],
            gate_ssem.at[layer, index],
            gate_rsem.at[layer, me_h],
            me_c,
            peer,
        )

    def gate_start(layer):
        for index, (dx, dc) in enumerate(head_steps):
            gate_copy(layer, dx, dc, index).start()
        gate_recv[layer][me_h] = gate_send[layer][me_h]

    def att_copy(layer, peer):
        return remote(
            att_send[layer].at[peer],
            att_recv[layer].at[me_h],
            att_ssem.at[layer, peer],
            att_rsem.at[layer, me_h],
            me_c,
            peer,
        )

    def attend(layer, user):
        per_user = HEADS // USERS
        acc[...] = jnp.zeros_like(acc)

        def body(i, carry):
            first = arr[layer][src[user * PAGES + 2 * i]]
            second = arr[layer][src[user * PAGES + 2 * i + 1]]
            keys = jnp.concatenate([first[:, :DH], second[:, :DH]], axis=0)
            values = jnp.concatenate([first[:, DH:], second[:, DH:]], axis=0)
            for r in range(per_user):
                score = lax.dot_general(
                    q_buf[user * per_user + r],
                    keys,
                    (((1,), (1,)), ((), ())),
                    preferred_element_type=F32,
                )
                weights = half_silu(score * (0.5 * DH**-0.5)).astype(BF16)
                acc[r] += jnp.dot(weights, values, preferred_element_type=F32)
            return carry

        lax.fori_loop(0, PAGES // 2, body, 0)
        scale = recip[user]
        for r in range(per_user):
            block = user * per_user + r
            own = jnp.sum(
                q_buf[block].astype(F32) * k_buf[block].astype(F32), axis=-1, keepdims=True
            )
            own = half_silu(own * (0.5 * DH**-0.5))
            total = (acc[r] + own * v_buf[block].astype(F32)) * scale
            att_send[layer][block] = total.astype(BF16)
        for r in range(per_user):
            block = user * per_user + r

            @pl.when(block != me_h)
            def _():
                att_copy(layer, block).start()

            @pl.when(block == me_h)
            def _():
                att_recv[layer][block] = att_send[layer][block]

    def finish(layer):
        for dx, dc in head_steps:
            source = head_peer(dx, dc)
            place = att_recv[layer].at[source]
            remote(
                place, place, att_ssem.at[layer, source], att_rsem.at[layer, source], me_c, source
            ).wait_recv()
            place = gate_recv[layer].at[source]
            remote(
                place, place, gate_ssem.at[layer, 0], gate_rsem.at[layer, source], me_c, source
            ).wait_recv()
        att = [att_recv[layer][h].astype(F32) for h in range(HEADS)]
        first = sum([jnp.sum(a, axis=-1, keepdims=True) for a in att]) * (1.0 / D)
        second = sum([jnp.sum(a * a, axis=-1, keepdims=True) for a in att]) * (1.0 / D)
        rstd = lax.rsqrt(second - first * first + 1e-05)
        update = state[...]
        for h in range(0, HEADS, 2):
            pair = [
                ((att[i] - first) * rstd * gate_recv[layer][i].astype(F32)).astype(BF16)
                for i in (h, h + 1)
            ]
            w_pair = jnp.concatenate([w_all[layer][h], w_all[layer][h + 1]], axis=0)
            update = update + jnp.dot(
                jnp.concatenate(pair, axis=1), w_pair, preferred_element_type=F32
            )
        return update

    def drain(layer):
        for i in range(NZ):
            for dy in range(1, NY):
                y_copy(layer, i, dy).wait_send()
            if OFFSETS[i] != 0:
                z_copy(layer, i).wait_send()
        rows_drain(layer)
        w_drain(layer)
        for index, (dx, dc) in enumerate(head_steps):
            gate_copy(layer, dx, dc, index).wait_send()
            att_copy(layer, head_peer(dx, dc)).wait_send()

    state[...] = cand[...].astype(F32)
    norm_rows(0)
    for layer in range(LAYERS):
        arr[layer][ZERO] = jnp.zeros((PAGE, 2 * DH), BF16)
    pl.semaphore_wait(barrier, NY - 1 + NZ - 1 + len(head_steps))

    def req_copy(dz):
        column = z_peer(dz)
        return remote(
            req_out.at[column],
            req_in.at[my_z],
            req_ssem.at[dz],
            req_rsem.at[my_z],
            my_y * NZ + column,
            me_h,
        )

    y_start(0, 0)
    for dz in range(1, NZ):
        req_copy(dz).start()
    req_in[my_z] = req_out[my_z]
    for i in range(1, NZ):
        y_start(0, i)
    rows_start(0)
    w_start()
    for dz in range(1, NZ):
        column = z_peer(dz)
        place = req_in.at[column]
        remote(
            place, place, req_ssem.at[dz], req_rsem.at[column], my_y * NZ + column, me_h
        ).wait_recv()
    to_smem = pltpu.make_async_copy(req_in, req_smem, smem_sem)
    to_smem.start()
    to_smem.wait()

    for i in range(NZ):
        pack_send(0, i)
        y_start(1, i)
    rows_wait(0)
    project(0)
    gate_start(0)
    for layer in range(LAYERS):
        w_forward(layer)
    for i in range(NZ):
        pack_send(1, i)
    for layer in range(LAYERS):
        for dz in range(1, NZ):
            z_wait(layer, dz)
        attend(layer, 0)
        attend(layer, 1)
        w_wait(layer)
        update = finish(layer)
        if layer + 1 < LAYERS:
            state[...] = update.astype(BF16).astype(F32)
            norm_rows(layer + 1)
            rows_start(layer + 1)
            rows_wait(layer + 1)
            project(layer + 1)
            gate_start(layer + 1)
        else:
            out[...] = update.astype(BF16)
    for layer in range(LAYERS):
        drain(layer)
    for dz in range(1, NZ):
        req_copy(dz).wait_send()


def both(shape, dtype=BF16):
    return [pltpu.VMEM(shape, dtype)] * LAYERS


def run(src, recip, cand, w_in, w_out, req, pool):
    dma = pltpu.SemaphoreType.DMA
    smem = pl.BlockSpec(memory_space=pltpu.SMEM)
    vmem = pl.BlockSpec(memory_space=pltpu.VMEM)
    return pl.pallas_call(
        kernel,
        out_shape=jax.ShapeDtypeStruct((BLOCK, D), BF16),
        in_specs=[smem, smem, vmem, vmem, vmem, vmem, pl.BlockSpec(memory_space=pl.ANY)],
        out_specs=vmem,
        scratch_shapes=[
            *both((NZ * C + 1, PAGE, 2 * DH)),
            *both((NZ - 1, C, PAGE, 2 * DH)),
            *both((HEADS, BLOCK, D)),
            *both((HEADS, DH, D)),
            *both((HEADS, BLOCK, DH)),
            *both((HEADS, BLOCK, DH)),
            *both((HEADS, BLOCK, DH)),
            *both((HEADS, BLOCK, DH)),
            *[pltpu.VMEM((2 * NY, PAGE, 2 * DH), BF16)] * (LAYERS * NZ),
            pltpu.VMEM((HEADS, BLOCK, DH), BF16),
            pltpu.VMEM((HEADS, BLOCK, DH), BF16),
            pltpu.VMEM((HEADS, BLOCK, DH), BF16),
            pltpu.VMEM((HEADS // USERS, BLOCK, DH), F32),
            pltpu.VMEM((BLOCK, D), F32),
            pltpu.VMEM((NZ, 1, 128), jnp.int32),
            pltpu.SMEM((NZ, 1, 128), jnp.int32),
            dma((LAYERS, NZ, NY)),
            dma((LAYERS, NZ, NY)),
            dma((LAYERS, NZ)),
            dma((LAYERS, NZ)),
            dma((NZ,)),
            dma((NZ,)),
            dma,
            dma((LAYERS, NX)),
            dma((LAYERS, NX)),
            dma((LAYERS, HEADS)),
            dma((LAYERS, NX)),
            dma((LAYERS, NX)),
            dma((LAYERS, HEADS)),
            dma((LAYERS, HEADS)),
            dma((LAYERS, HEADS)),
            dma((LAYERS, HEADS)),
            dma((LAYERS, HEADS)),
        ],
        compiler_params=pltpu.CompilerParams(
            collective_id=0, has_side_effects=True, vmem_limit_bytes=62 * 2**20
        ),
    )(src, recip, cand, w_in, w_out, req, pool)


def shards(candidates, proj_in, proj_out, page_pool, page_owner, history_pages):
    owners = page_owner.reshape(-1)
    count = owners.shape[0]
    order = jnp.arange(count)
    before = order[None, :] < order[:, None]
    slots = jnp.sum(((owners[:, None] == owners[None, :]) & before).astype(jnp.int32), axis=1)
    live = (jnp.arange(PAGES)[None, :] < history_pages[:, None]).reshape(-1)
    column = owners % NZ
    rank = jnp.sum(
        ((column[:, None] == column[None, :]) & before & live[None, :]).astype(jnp.int32), axis=1
    )
    place = (owners // NZ) * 2 + slots
    src = jnp.where(live, column * C + rank, ZERO).astype(jnp.int32)
    chosen = (src[None, :] == jnp.arange(NZ * C)[:, None]).astype(jnp.int32)
    req = jnp.sum(chosen * place[None, :], axis=1).reshape(NZ, 1, C)
    req = jnp.pad(req, ((0, 0), (0, 0), (0, 128 - C))).astype(jnp.int32)
    recip = 1.0 / (history_pages * PAGE + 1).astype(F32)
    return run(src, recip, candidates, proj_in, proj_out, req, page_pool[0])


def solution(mesh):
    return jax.shard_map(
        shards,
        mesh=mesh,
        in_specs=(
            P(("cache", "head"), None),
            P(None, None, "head"),
            P(None, "head", None),
            P("cache", None, None, None, None, "head"),
            P("cache", None, None),
            P("cache"),
        ),
        out_specs=P(("cache", "head"), None),
        check_vma=False,
    )
```

time: 457 us -> 232 us (0.51)
  waiting for transfers between devices: 266 us -> 0 us
  Pallas kernels: 0 us -> 225 us
  local copies, waits for them, and re-layouts: 64 us -> 3.24 us
  blocking collectives: 45.8 us -> 0 us
  matrix products: 41.9 us -> 0 us
  between operations: 13.3 us -> 0.03 us
  starting transfers between devices: 11.8 us -> 0 us
  other arithmetic: 11.8 us -> 3.71 us
    pallas_call x0 -> x1, Pallas kernels: none -> 225 us  [run(): pl.pallas_call(kernel, out_shape=jax.ShapeDtypeStruct((BLOCK, D), BF16),...]
    all_to_all x1 -> x0, waiting for transfers between devices: 129 us -> none  [shards(): lax.all_to_all(pool_local, 'cache', split_axis=0, concat_axis=0, tiled=True)]
    reduce_scatter x2 -> x0, waiting for transfers between devices: 85.4 us -> none  [hstu_layer(): lax.psum_scatter(jnp.dot(gated, w_out, preferred_element_type=jnp.float32...]
    all_gather x2 -> x0, waiting for transfers between devices: 51.4 us -> none  [hstu_layer(): lax.all_gather(normed, 'head', axis=0, tiled=True)]
    psum x2 -> x0, blocking collectives: 45.8 us -> none  [hstu_layer(): lax.psum((jnp.sum(attended, axis=-1), jnp.sum(attended * attended, axis=-...]
    dot_general x6 -> x0, matrix products: 41.9 us -> none  [the longest x2 20.4 us: hstu_layer(): jnp.einsum('uhce,uehd->uchd', weights, hist_value, preferred_element_type...]
    slice x5 -> x0, local copies, waits for them, and re-layouts: 23.4 us -> none  [the longest x2 9 us: hstu_layer(): gate = act[:, :, :, 0, :]]
    unnamed x23 -> x4, local copies, waits for them, and re-layouts: 21.2 us -> 2.38 us
  transfers between devices with their start and end apart: 5 -> 0, of which waited for: 5 -> 0; matrix products, arithmetic and copies ran while one was open for 9% -> 0% of each run, Pallas kernels for 0% -> 0%
where the time goes in v1:
time: 232 us
  Pallas kernels  225 us (97%)
  other arithmetic  3.71 us (2%)
  local copies, waits for them, and re-layouts  3.24 us (1%)
    pallas_call x1, Pallas kernels, run(): pl.pallas_call(kernel, out_shape=jax.ShapeDtypeStruct((BLOCK, D), BF16),...  225 us

profile of v1, /device:TPU:7, one launch (start us, length us, event | category | flops | bytes accessed | tf_op | source)
XLA Modules:
  0.0 232.0 jit_solution(5017459782242058616)
XLA Ops:
  0.0 0.5 broadcast.153
  0.5 1.3 reduce.3
  1.9 0.1 reshape.118
  1.9 0.2 convert_reduce_fusion
  2.1 1.2 convert_divide_fusion.recip
  3.3 0.7 iota_compare_fusion.2
  4.0 0.1 lt.52
  4.1 0.2 convert_reduce_fusion.1
  4.3 0.0 copy-start
  4.3 0.1 select_reduce_fusion
  4.4 0.1 reshape.119
  4.5 0.6 pad.4.req_out
  5.1 0.0 copy-done
  5.1 225.0 %shard_map.64 = bf16[256,1024]{1,0:T(8,128)(2,1)} custom-call(s32[32]{0:T(128)} %copy-done, f32[2]{0:T(128)} %convert_divide_fusion.recip, bf16[256,1024]{1,0:T(8,128)(2,1)} %cand.1, bf16[2,1024,512]{2,1,0:T(8,128)(2,1)} %w_in.1, bf16[2,128,1024]{2,1,0:T(8,128)(2,1)} %w_out.1, s32[8,1,128]{2,1,0:T(1,128)} %pad.4.req_out, bf16[32,2,2,128,256]{4,3,2,1,0:T(8,128)(2,1)} %bitcast.3), custom_call_target="tpu_custom_call" | custom-call | tf_op jit(solution)/shard_map/pallas_call | solution.py:491
  230.1 1.9 copy.10
  (2 shorter events, 0.0 us)
Async XLA Ops:
  4.3 0.8 copy-start

commit v2 on v1

--- a/solution.py
+++ b/solution.py
@@ -1,3 +1,5 @@
+import functools
+
 import jax
 import jax.numpy as jnp
 from jax import lax
@@ -17,9 +19,8 @@
 NX = 4
 HEADS = 8
 BLOCK = 256
-C = 8
-ZERO = NZ * C
-REQ = 16
+CAPS = (6, 8)
+WINDOW = 3
 OFFSETS = (4, 3, 5, 2, 6, 1, 7, 0)
 F32 = jnp.float32
 BF16 = jnp.bfloat16
@@ -30,14 +31,15 @@
 
 
 def kernel(
-    src,
-    recip,
+    C,
+    lengths,
+    owners,
     cand,
     w_in,
     w_out,
-    req_out,
     pool,
     out,
+    overflow,
     *scratch,
 ):
     (
@@ -57,14 +59,23 @@
         v_buf,
         acc,
         state,
+        req_out,
         req_in,
         req_smem,
+        src_vmem,
+        src,
+        flag_out,
+        flag_in,
+        flag_all,
+        flag_smem,
         y_ssem,
         y_rsem,
         z_ssem,
         z_rsem,
         req_ssem,
         req_rsem,
+        flag_ssem,
+        flag_rsem,
         smem_sem,
         row_ssem,
         row_fsem,
@@ -78,6 +89,7 @@
         att_rsem,
     ) = scratch[32:]
 
+    ZERO = NZ * C
     me_c = lax.axis_index("cache")
     me_h = lax.axis_index("head")
     my_y = me_c // NZ
@@ -121,79 +133,50 @@
             device_id_type=MESH,
         )
 
-    def y_copy(layer, i, dy):
-        group = y_peer(dy) * NZ + z_peer(OFFSETS[i])
-        return remote(
-            pool.at[group, :, layer],
-            ybuf[layer * NZ + i].at[pl.ds(my_y * 2, 2)],
-            y_ssem.at[layer, i, dy],
-            y_rsem.at[layer, i, my_y],
-            y_peer(dy) * NZ + my_z,
-            me_h,
-        )
-
-    def y_local(layer, i):
-        group = my_y * NZ + z_peer(OFFSETS[i])
-        return pltpu.make_async_copy(
-            pool.at[group, :, layer],
-            ybuf[layer * NZ + i].at[pl.ds(my_y * 2, 2)],
-            y_rsem.at[layer, i, my_y],
-        )
-
-    def y_start(layer, i):
+    def wait_bytes(ref, sem):
+        pltpu.make_async_copy(ref, ref, sem).wait()
+
+    def y_start(n):
+        layer, i = divmod(n, NZ)
+        column = z_peer(OFFSETS[i])
+        place = ybuf[n].at[pl.ds(my_y * 2, 2)]
         for dy in (2, 1, 3):
-            y_copy(layer, i, dy).start()
-        y_local(layer, i).start()
-
-    def y_wait(layer, i):
-        for dy in range(1, NY):
-            other = y_peer(dy)
-            place = ybuf[layer * NZ + i].at[pl.ds(other * 2, 2)]
-            remote(
+            remote(
+                pool.at[y_peer(dy) * NZ + column, :, layer],
                 place,
-                place,
-                y_ssem.at[layer, i, dy],
-                y_rsem.at[layer, i, other],
-                other * NZ + my_z,
+                y_ssem.at[layer],
+                y_rsem.at[n],
+                y_peer(dy) * NZ + my_z,
                 me_h,
-            ).wait_recv()
-        y_local(layer, i).wait()
-
-    def z_copy(layer, i):
+            ).start()
+        pltpu.make_async_copy(
+            pool.at[my_y * NZ + column, :, layer], place, y_rsem.at[n]
+        ).start()
+
+    def pack_send(n):
+        if n + WINDOW < LAYERS * NZ:
+            y_start(n + WINDOW)
+        layer, i = divmod(n, NZ)
+        wait_bytes(ybuf[n], y_rsem.at[n])
         column = z_peer(OFFSETS[i])
-        return remote(
-            pack[layer].at[i],
-            arr[layer].at[pl.ds(my_z * C, C)],
-            z_ssem.at[layer, i],
-            z_rsem.at[layer, my_z],
-            my_y * NZ + column,
-            me_h,
-        )
-
-    def z_wait(layer, dz):
-        column = z_peer(dz)
-        place = arr[layer].at[pl.ds(column * C, C)]
-        remote(
-            place,
-            place,
-            z_ssem.at[layer, 0],
-            z_rsem.at[layer, column],
-            my_y * NZ + column,
-            me_h,
-        ).wait_recv()
-
-    def pack_send(layer, i):
-        y_wait(layer, i)
-        column = z_peer(OFFSETS[i])
-        buf = ybuf[layer * NZ + i]
         for j in range(C):
-            page = buf[req_smem[column, 0, j]]
+            page = ybuf[n][jnp.clip(req_smem[column, 0, j], 0, 2 * NY - 1)]
             if OFFSETS[i] == 0:
                 arr[layer][my_z * C + j] = page
             else:
                 pack[layer][i, j] = page
         if OFFSETS[i] != 0:
-            z_copy(layer, i).start()
+            remote(
+                pack[layer].at[i],
+                arr[layer].at[pl.ds(my_z * C, C)],
+                z_ssem.at[layer],
+                z_rsem.at[layer],
+                my_y * NZ + column,
+                me_h,
+            ).start()
+
+    def z_wait(layer):
+        wait_bytes(arr[layer].at[pl.ds(0, (NZ - 1) * C)], z_rsem.at[layer])
 
     def rows_start(layer):
         place = rows_all[layer].at[me_h]
@@ -307,28 +290,25 @@
 
         lax.fori_loop(0, HEADS, body, 0)
 
-    def gate_copy(layer, dx, dc, index):
-        peer = head_peer(dx, dc)
-        return remote(
-            gate_send[layer].at[peer],
-            gate_recv[layer].at[me_h],
-            gate_ssem.at[layer, index],
-            gate_rsem.at[layer, me_h],
-            me_c,
-            peer,
-        )
-
     def gate_start(layer):
-        for index, (dx, dc) in enumerate(head_steps):
-            gate_copy(layer, dx, dc, index).start()
+        for dx, dc in head_steps:
+            peer = head_peer(dx, dc)
+            remote(
+                gate_send[layer].at[peer],
+                gate_recv[layer].at[me_h],
+                gate_ssem.at[layer],
+                gate_rsem.at[layer],
+                me_c,
+                peer,
+            ).start()
         gate_recv[layer][me_h] = gate_send[layer][me_h]
 
     def att_copy(layer, peer):
         return remote(
             att_send[layer].at[peer],
             att_recv[layer].at[me_h],
-            att_ssem.at[layer, peer],
-            att_rsem.at[layer, me_h],
+            att_ssem.at[layer],
+            att_rsem.at[layer],
             me_c,
             peer,
         )
@@ -338,8 +318,9 @@
         acc[...] = jnp.zeros_like(acc)
 
         def body(i, carry):
-            first = arr[layer][src[user * PAGES + 2 * i]]
-            second = arr[layer][src[user * PAGES + 2 * i + 1]]
+            first, second = [
+                arr[layer][jnp.clip(src[user * PAGES + 2 * i + k, 0], 0, ZERO)] for k in (0, 1)
+            ]
             keys = jnp.concatenate([first[:, :DH], second[:, :DH]], axis=0)
             values = jnp.concatenate([first[:, DH:], second[:, DH:]], axis=0)
             for r in range(per_user):
@@ -354,7 +335,7 @@
             return carry
 
         lax.fori_loop(0, PAGES // 2, body, 0)
-        scale = recip[user]
+        scale = 1.0 / jnp.full((1, DH), lengths[user] * PAGE + 1, jnp.int32).astype(F32)
         for r in range(per_user):
             block = user * per_user + r
             own = jnp.sum(
@@ -375,16 +356,8 @@
                 att_recv[layer][block] = att_send[layer][block]
 
     def finish(layer):
-        for dx, dc in head_steps:
-            source = head_peer(dx, dc)
-            place = att_recv[layer].at[source]
-            remote(
-                place, place, att_ssem.at[layer, source], att_rsem.at[layer, source], me_c, source
-            ).wait_recv()
-            place = gate_recv[layer].at[source]
-            remote(
-                place, place, gate_ssem.at[layer, 0], gate_rsem.at[layer, source], me_c, source
-            ).wait_recv()
+        wait_bytes(gate_recv[layer].at[pl.ds(0, HEADS - 1)], gate_rsem.at[layer])
+        wait_bytes(att_recv[layer].at[pl.ds(0, HEADS - 1)], att_rsem.at[layer])
         att = [att_recv[layer][h].astype(F32) for h in range(HEADS)]
         first = sum([jnp.sum(a, axis=-1, keepdims=True) for a in att]) * (1.0 / D)
         second = sum([jnp.sum(a * a, axis=-1, keepdims=True) for a in att]) * (1.0 / D)
@@ -402,97 +375,155 @@
         return update
 
     def drain(layer):
-        for i in range(NZ):
-            for dy in range(1, NY):
-                y_copy(layer, i, dy).wait_send()
-            if OFFSETS[i] != 0:
-                z_copy(layer, i).wait_send()
+        wait_bytes(gate_send[layer].at[pl.ds(0, HEADS - 1)], gate_ssem.at[layer])
+        wait_bytes(att_send[layer].at[pl.ds(0, HEADS - 1)], att_ssem.at[layer])
+        wait_bytes(arr[layer].at[pl.ds(0, NZ * (NY - 1) * 2)], y_ssem.at[layer])
+        wait_bytes(pack[layer], z_ssem.at[layer])
         rows_drain(layer)
         w_drain(layer)
-        for index, (dx, dc) in enumerate(head_steps):
-            gate_copy(layer, dx, dc, index).wait_send()
-            att_copy(layer, head_peer(dx, dc)).wait_send()
+
+    def make_requests():
+        count = USERS * PAGES
+        lane = lax.broadcasted_iota(jnp.int32, (count, count), 1)
+        sub = lax.broadcasted_iota(jnp.int32, (count, count), 0)
+        before = lane < sub
+        row = jnp.zeros((1, count), jnp.int32)
+        col = jnp.zeros((count, 1), jnp.int32)
+        for p in range(count):
+            owner = owners[p // PAGES, 0, p % PAGES]
+            row = jnp.where(lane[:1] == p, owner, row)
+            col = jnp.where(sub[:, :1] == p, owner, col)
+
+        def live_of(index):
+            length = jnp.where(index < PAGES, lengths[0], lengths[1])
+            return lax.rem(index, PAGES) < length
+
+        def total(mask, axis):
+            return jnp.sum(mask.astype(jnp.int32), axis=axis, keepdims=True)
+
+        slot = jnp.minimum(total((row == col) & before, 1), 1)
+        near = (lax.rem(row, NZ) == lax.rem(col, NZ)) & before & live_of(lane)
+        rank = total(near, 1)
+        live = live_of(lax.broadcasted_iota(jnp.int32, (count, 1), 0))
+        place = lax.rem(col // NZ, NY) * 2 + slot
+        target = jnp.where(live & (rank < C), lax.rem(col, NZ) * C + rank, ZERO)
+        src_vmem[...] = jnp.broadcast_to(target, (count, 128))
+        over = jnp.max((live & (rank >= C)).astype(jnp.int32), axis=0, keepdims=True)
+        lanes = lax.broadcasted_iota(jnp.int32, (count, 128), 1)
+        for z in range(NZ):
+            hit = (target == lanes + z * C) & (target < ZERO) & (lanes < C)
+            line = jnp.sum(jnp.where(hit, place, 0), axis=0, keepdims=True)
+            line = jnp.where(lanes[:1] == 127, over, line)
+            req_out[z] = line
 
     state[...] = cand[...].astype(F32)
     norm_rows(0)
+    make_requests()
     for layer in range(LAYERS):
         arr[layer][ZERO] = jnp.zeros((PAGE, 2 * DH), BF16)
     pl.semaphore_wait(barrier, NY - 1 + NZ - 1 + len(head_steps))
 
-    def req_copy(dz):
+    y_start(0)
+    for dz in range(1, NZ):
         column = z_peer(dz)
-        return remote(
+        remote(
             req_out.at[column],
             req_in.at[my_z],
-            req_ssem.at[dz],
-            req_rsem.at[my_z],
+            req_ssem,
+            req_rsem,
             my_y * NZ + column,
             me_h,
-        )
-
-    y_start(0, 0)
-    for dz in range(1, NZ):
-        req_copy(dz).start()
+        ).start()
     req_in[my_z] = req_out[my_z]
-    for i in range(1, NZ):
-        y_start(0, i)
+    for n in range(1, WINDOW):
+        y_start(n)
     rows_start(0)
-    w_start()
-    for dz in range(1, NZ):
-        column = z_peer(dz)
-        place = req_in.at[column]
+    src_copy = pltpu.make_async_copy(src_vmem, src, smem_sem.at[1])
+    src_copy.start()
+    wait_bytes(req_in.at[pl.ds(0, NZ - 1)], req_rsem)
+    to_smem = pltpu.make_async_copy(req_in, req_smem, smem_sem.at[0])
+    to_smem.start()
+    flag_out[0] = jnp.max(req_in[...], axis=0)
+    for dy in range(1, NY):
         remote(
-            place, place, req_ssem.at[dz], req_rsem.at[column], my_y * NZ + column, me_h
-        ).wait_recv()
-    to_smem = pltpu.make_async_copy(req_in, req_smem, smem_sem)
-    to_smem.start()
+            flag_out.at[0],
+            flag_in.at[my_y],
+            flag_ssem,
+            flag_rsem,
+            y_peer(dy) * NZ + my_z,
+            me_h,
+        ).start()
+    flag_in[my_y] = flag_out[0]
     to_smem.wait()
-
-    for i in range(NZ):
-        pack_send(0, i)
-        y_start(1, i)
+    src_copy.wait()
+
+    for n in range(6):
+        pack_send(n)
     rows_wait(0)
     project(0)
     gate_start(0)
+    w_start()
+    for n in range(6, 11):
+        pack_send(n)
     for layer in range(LAYERS):
         w_forward(layer)
-    for i in range(NZ):
-        pack_send(1, i)
+    pack_send(11)
+    z_wait(0)
+    attend(0, 0)
+    attend(0, 1)
+    pack_send(12)
     for layer in range(LAYERS):
-        for dz in range(1, NZ):
-            z_wait(layer, dz)
-        attend(layer, 0)
-        attend(layer, 1)
         w_wait(layer)
-        update = finish(layer)
-        if layer + 1 < LAYERS:
-            state[...] = update.astype(BF16).astype(F32)
-            norm_rows(layer + 1)
-            rows_start(layer + 1)
-            rows_wait(layer + 1)
-            project(layer + 1)
-            gate_start(layer + 1)
-        else:
-            out[...] = update.astype(BF16)
-    for layer in range(LAYERS):
-        drain(layer)
-    for dz in range(1, NZ):
-        req_copy(dz).wait_send()
+    update = finish(0)
+    state[...] = update.astype(BF16).astype(F32)
+    norm_rows(1)
+    rows_start(1)
+    for n in range(13, 15):
+        pack_send(n)
+    rows_wait(1)
+    project(1)
+    gate_start(1)
+    pack_send(15)
+    drain(0)
+    wait_bytes(req_in.at[pl.ds(0, NZ - 1)], req_ssem)
+    wait_bytes(flag_in.at[pl.ds(0, NY - 1)], flag_rsem)
+    wait_bytes(flag_in.at[pl.ds(0, NY - 1)], flag_ssem)
+    flag_all[...] = jnp.max(flag_in[...], axis=0)
+    to_smem = pltpu.make_async_copy(flag_all, flag_smem, smem_sem.at[0])
+    to_smem.start()
+    to_smem.wait()
+    overflow[0] = flag_smem[0, 127]
+    z_wait(1)
+    attend(1, 0)
+    attend(1, 1)
+    out[...] = finish(1).astype(BF16)
+    drain(1)
 
 
 def both(shape, dtype=BF16):
     return [pltpu.VMEM(shape, dtype)] * LAYERS
 
 
-def run(src, recip, cand, w_in, w_out, req, pool):
+def run(turn, lengths, owners, cand, w_in, w_out, pool):
+    C = CAPS[turn]
     dma = pltpu.SemaphoreType.DMA
+    vmem = pl.BlockSpec(memory_space=pltpu.VMEM)
     smem = pl.BlockSpec(memory_space=pltpu.SMEM)
-    vmem = pl.BlockSpec(memory_space=pltpu.VMEM)
     return pl.pallas_call(
-        kernel,
-        out_shape=jax.ShapeDtypeStruct((BLOCK, D), BF16),
-        in_specs=[smem, smem, vmem, vmem, vmem, vmem, pl.BlockSpec(memory_space=pl.ANY)],
-        out_specs=vmem,
+        functools.partial(kernel, C),
+        out_shape=(
+            jax.ShapeDtypeStruct((BLOCK, D), BF16),
+            jax.ShapeDtypeStruct((1,), jnp.int32),
+        ),
+        in_specs=[
+            smem,
+            smem,
+            vmem,
+            vmem,
+            vmem,
+            pl.BlockSpec(memory_space=pl.ANY),
+        ],
+        out_specs=(vmem, smem),
         scratch_shapes=[
             *both((NZ * C + 1, PAGE, 2 * DH)),
             *both((NZ - 1, C, PAGE, 2 * DH)),
@@ -509,49 +540,45 @@
             pltpu.VMEM((HEADS // USERS, BLOCK, DH), F32),
             pltpu.VMEM((BLOCK, D), F32),
             pltpu.VMEM((NZ, 1, 128), jnp.int32),
+            pltpu.VMEM((NZ, 1, 128), jnp.int32),
             pltpu.SMEM((NZ, 1, 128), jnp.int32),
-            dma((LAYERS, NZ, NY)),
-            dma((LAYERS, NZ, NY)),
-            dma((LAYERS, NZ)),
-            dma((LAYERS, NZ)),
-            dma((NZ,)),
-            dma((NZ,)),
+            pltpu.VMEM((USERS * PAGES, 128), jnp.int32),
+            pltpu.SMEM((USERS * PAGES, 128), jnp.int32),
+            pltpu.VMEM((1, 1, 128), jnp.int32),
+            pltpu.VMEM((NY, 1, 128), jnp.int32),
+            pltpu.VMEM((1, 128), jnp.int32),
+            pltpu.SMEM((1, 128), jnp.int32),
+            dma((LAYERS,)),
+            dma((LAYERS * NZ,)),
+            dma((LAYERS,)),
+            dma((LAYERS,)),
             dma,
+            dma,
+            dma,
+            dma,
+            dma((2,)),
             dma((LAYERS, NX)),
             dma((LAYERS, NX)),
             dma((LAYERS, HEADS)),
             dma((LAYERS, NX)),
             dma((LAYERS, NX)),
             dma((LAYERS, HEADS)),
-            dma((LAYERS, HEADS)),
-            dma((LAYERS, HEADS)),
-            dma((LAYERS, HEADS)),
-            dma((LAYERS, HEADS)),
+            dma((LAYERS,)),
+            dma((LAYERS,)),
+            dma((LAYERS,)),
+            dma((LAYERS,)),
         ],
         compiler_params=pltpu.CompilerParams(
-            collective_id=0, has_side_effects=True, vmem_limit_bytes=62 * 2**20
+            collective_id=turn, has_side_effects=True, vmem_limit_bytes=62 * 2**20
         ),
-    )(src, recip, cand, w_in, w_out, req, pool)
+    )(lengths, owners, cand, w_in, w_out, pool)
 
 
 def shards(candidates, proj_in, proj_out, page_pool, page_owner, history_pages):
-    owners = page_owner.reshape(-1)
-    count = owners.shape[0]
-    order = jnp.arange(count)
-    before = order[None, :] < order[:, None]
-    slots = jnp.sum(((owners[:, None] == owners[None, :]) & before).astype(jnp.int32), axis=1)
-    live = (jnp.arange(PAGES)[None, :] < history_pages[:, None]).reshape(-1)
-    column = owners % NZ
-    rank = jnp.sum(
-        ((column[:, None] == column[None, :]) & before & live[None, :]).astype(jnp.int32), axis=1
-    )
-    place = (owners // NZ) * 2 + slots
-    src = jnp.where(live, column * C + rank, ZERO).astype(jnp.int32)
-    chosen = (src[None, :] == jnp.arange(NZ * C)[:, None]).astype(jnp.int32)
-    req = jnp.sum(chosen * place[None, :], axis=1).reshape(NZ, 1, C)
-    req = jnp.pad(req, ((0, 0), (0, 0), (0, 128 - C))).astype(jnp.int32)
-    recip = 1.0 / (history_pages * PAGE + 1).astype(F32)
-    return run(src, recip, candidates, proj_in, proj_out, req, page_pool[0])
+    owners = page_owner.transpose(0, 2, 1)
+    args = (history_pages, owners, candidates, proj_in, proj_out, page_pool[0])
+    first, overflow = run(0, *args)
+    return lax.switch(overflow[0], [lambda: first, lambda: run(1, *args)[0]])
 
 
 def solution(mesh):

time: 232 us -> 186 us (0.80); the launches traced: 232 us -> 183 us
  Pallas kernels: 225 us -> 181 us
  other arithmetic: 3.71 us -> 0 us
  local copies, waits for them, and re-layouts: 3.24 us -> 0.81 us
    pallas_call x1, Pallas kernels: 225 us -> 181 us  [run(): pl.pallas_call(functools.partial(kernel, C), out_shape=(jax.ShapeDtypeStr...]
where the time goes in v2:
time: 186 us; the launch traced here: 183 us
  Pallas kernels  181 us (97%)
    pallas_call x1, Pallas kernels, run(): pl.pallas_call(functools.partial(kernel, C), out_shape=(jax.ShapeDtypeStr...  181 us

profile of v2, /device:TPU:7, one launch (start us, length us, event | category | flops | bytes accessed | tf_op | source)
XLA Modules:
  0.0 183.1 jit_solution(13369680661082343366)
XLA Ops:
  0.0 0.0 copy-start.3
  0.0 0.0 copy-start.2
  0.0 0.0 copy-start.1
  0.0 0.0 copy-start
  0.0 181.4 %shard_map.66 = (bf16[256,1024]{1,0:T(8,128)(2,1)S(1)}, s32[1]{0:T(128)}) custom-call(s32[2]{0:T(128)} %lengths.1, s32[2,1,16]{2,1,0:T(1,128)} %bitcast.8, bf16[256,1024]{1,0:T(8,128)(2,1)} %cand.1, bf16[2,1024,512]{2,1,0:T(8,128)(2,1)} %w_in.1, bf16[2,128,1024]{2,1,0:T(8,128)(2,1)} %w_out.1, bf16[32,2,2,128,256]{4,3,2,1,0:T(8,128)(2,1)} %bitcast.6), custom_call_target="tpu_custom_call" | custom-call | tf_op jit(solution)/shard_map/pallas_call | solution.py:512
  182.0 0.0 copy-done.3
  182.0 0.0 copy-done.2
  182.0 0.0 copy-done.1
  182.0 0.0 copy-done
  182.0 0.2 conditional.1
  182.3 0.8 copy.14
Async XLA Ops:
  0.0 182.0 %copy-start.3 = (s32[2]{0:T(128)S(1)}, s32[2]{0:T(128)}, u32[]{:S(2)}) copy-start(s32[2]{0:T(128)} %lengths.1) | copy-start | bytes 28
  0.0 182.0 %copy-start.2 = (s32[2,16,1]{1,2,0:T(1,128)S(1)}, s32[2,16,1]{1,2,0:T(1,128)}, u32[]{:S(2)}) copy-start(s32[2,16,1]{1,2,0:T(1,128)} %param.12) | copy-start | bytes 388
  0.0 182.0 %copy-start.1 = (bf16[2,128,1024]{2,1,0:T(8,128)(2,1)S(1)}, bf16[2,128,1024]{2,1,0:T(8,128)(2,1)}, u32[]{:S(2)}) copy-start(bf16[2,128,1024]{2,1,0:T(8,128)(2,1)} %w_out.1) | copy-start | bytes 1572868
  0.0 182.0 %copy-start = (bf16[256,1024]{1,0:T(8,128)(2,1)S(1)}, bf16[256,1024]{1,0:T(8,128)(2,1)}, u32[]{:S(2)}) copy-start(bf16[256,1024]{1,0:T(8,128)(2,1)} %cand.1) | copy-start | bytes 1572868

commit v3 on v2

--- a/solution.py
+++ b/solution.py
@@ -45,19 +45,22 @@
     (
         arr,
         pack,
-        rows_all,
         w_all,
-        gate_send,
         gate_recv,
+        q_buf,
         att_send,
         att_recv,
-    ) = [scratch[2 * i : 2 * i + 2] for i in range(8)]
-    ybuf = scratch[16:32]
+    ) = [scratch[2 * i : 2 * i + 2] for i in range(7)]
+    ybuf = scratch[14:30]
     (
-        q_buf,
+        rows_all,
+        w_next,
         k_buf,
         v_buf,
-        acc,
+        own_buf,
+        out_send,
+        keys,
+        values,
         state,
         req_out,
         req_in,
@@ -77,17 +80,13 @@
         flag_ssem,
         flag_rsem,
         smem_sem,
-        row_ssem,
-        row_fsem,
-        row_rsem,
-        w_ssem,
-        w_fsem,
-        w_rsem,
-        gate_ssem,
-        gate_rsem,
+        spread_ssem,
+        spread_rsem,
+        cross_ssem,
+        cross_rsem,
         att_ssem,
         att_rsem,
-    ) = scratch[32:]
+    ) = scratch[30:]
 
     ZERO = NZ * C
     me_c = lax.axis_index("cache")
@@ -178,130 +177,96 @@
     def z_wait(layer):
         wait_bytes(arr[layer].at[pl.ds(0, (NZ - 1) * C)], z_rsem.at[layer])
 
-    def rows_start(layer):
-        place = rows_all[layer].at[me_h]
+    def spread_start(k, block, places):
         for dx in (2, 1, 3):
             remote(
-                place,
-                place,
-                row_ssem.at[layer, dx],
-                row_rsem.at[layer, me_h],
+                block,
+                places.at[me_h],
+                spread_ssem.at[k],
+                spread_rsem.at[k, me_h],
                 me_c,
                 head_peer(dx, 0),
             ).start()
         remote(
-            place, place, row_ssem.at[layer, 0], row_rsem.at[layer, me_h], me_c, sibling
+            block, places.at[me_h], spread_ssem.at[k], spread_rsem.at[k, me_h], me_c, sibling
         ).start()
 
-    def rows_wait(layer):
+    def spread_forward(k, places):
         for dx in (1, 3, 2):
             source = head_peer(dx, 0)
-            place = rows_all[layer].at[source]
-            copy = remote(
-                place, place, row_fsem.at[layer, dx], row_rsem.at[layer, source], me_c, sibling
-            )
-            copy.wait_recv()
-            copy.start()
+            place = places.at[source]
+            wait_bytes(place, spread_rsem.at[k, source])
+            remote(
+                place, place, spread_ssem.at[k], spread_rsem.at[k, source], me_c, sibling
+            ).start()
+
+    def spread_wait(k, places):
         for dx in (0, 1, 3, 2):
             source = head_peer(dx, 1)
-            place = rows_all[layer].at[source]
-            remote(
-                place, place, row_fsem.at[layer, dx], row_rsem.at[layer, source], me_c, sibling
-            ).wait_recv()
-
-    def rows_drain(layer):
-        place = rows_all[layer].at[me_h]
-        for dx in range(NX):
-            remote(
-                place, place, row_ssem.at[layer, dx], row_rsem.at[layer, me_h], me_c, sibling
-            ).wait_send()
-        for dx in range(1, NX):
-            remote(
-                place, place, row_fsem.at[layer, dx], row_rsem.at[layer, me_h], me_c, sibling
-            ).wait_send()
-
-    def w_place(layer, source):
-        return w_all[layer].at[source]
-
-    def w_start():
-        for layer in range(LAYERS):
-            for dx in (2, 1, 3):
-                remote(
-                    w_out.at[layer],
-                    w_place(layer, me_h),
-                    w_ssem.at[layer, dx],
-                    w_rsem.at[layer, me_h],
-                    me_c,
-                    head_peer(dx, 0),
-                ).start()
-            remote(
-                w_out.at[layer],
-                w_place(layer, me_h),
-                w_ssem.at[layer, 0],
-                w_rsem.at[layer, me_h],
-                me_c,
-                sibling,
-            ).start()
-            w_all[layer][me_h] = w_out[layer]
-
-    def w_forward(layer):
-        for dx in (1, 3, 2):
-            source = head_peer(dx, 0)
-            place = w_place(layer, source)
-            copy = remote(
-                place, place, w_fsem.at[layer, dx], w_rsem.at[layer, source], me_c, sibling
-            )
-            copy.wait_recv()
-            copy.start()
-
-    def w_wait(layer):
-        for dx in range(NX):
-            source = head_peer(dx, 1)
-            place = w_place(layer, source)
-            remote(
-                place, place, w_fsem.at[layer, dx], w_rsem.at[layer, source], me_c, sibling
-            ).wait_recv()
-
-    def w_drain(layer):
-        place = w_place(layer, me_h)
-        for dx in range(NX):
-            remote(
-                place, place, w_ssem.at[layer, dx], w_rsem.at[layer, me_h], me_c, sibling
-            ).wait_send()
-        for dx in range(1, NX):
-            remote(
-                place, place, w_fsem.at[layer, dx], w_rsem.at[layer, me_h], me_c, sibling
-            ).wait_send()
-
-    def norm_rows(layer):
+            wait_bytes(places.at[source], spread_rsem.at[k, source])
+
+    def spread_drain(k, places):
+        wait_bytes(places.at[pl.ds(0, HEADS - 1)], spread_ssem.at[k])
+
+    def normed_rows():
         xf = state[...]
         normed = xf * lax.rsqrt(jnp.mean(xf * xf, axis=-1, keepdims=True) + 1e-06)
-        rows_all[layer][me_h] = normed.astype(BF16)
-
-    def project(layer):
+        return normed.astype(BF16)
+
+    def activations(rows, w):
+        act = jnp.dot(rows, w, preferred_element_type=F32)
+        act = half_silu(act * 0.5).astype(BF16)
+        return [act[:, i * DH : (i + 1) * DH] for i in range(4)]
+
+    def reciprocal(user):
+        return 1.0 / jnp.full((1, DH), lengths[user] * PAGE + 1, jnp.int32).astype(F32)
+
+    def own_term(query, key, value):
+        own = jnp.sum(query.astype(F32) * key.astype(F32), axis=-1, keepdims=True)
+        return half_silu(own * (0.5 * DH**-0.5)) * value.astype(F32)
+
+    def project_head():
         def body(i, carry):
-            act = jnp.dot(rows_all[layer][i], w_in[layer], preferred_element_type=F32)
-            act = half_silu(act * 0.5).astype(BF16)
-            gate_send[layer][i] = act[:, :DH]
-            v_buf[i] = act[:, DH : 2 * DH]
-            q_buf[i] = act[:, 2 * DH : 3 * DH]
-            k_buf[i] = act[:, 3 * DH :]
+            gate, value, query, key = activations(rows_all[i], w_in[0])
+            out_send[0, i] = gate
+            v_buf[i] = value
+            q_buf[0][i] = query
+            k_buf[i] = key
             return carry
 
         lax.fori_loop(0, HEADS, body, 0)
-
-    def gate_start(layer):
         for dx, dc in head_steps:
-            peer = head_peer(dx, dc)
-            remote(
-                gate_send[layer].at[peer],
-                gate_recv[layer].at[me_h],
-                gate_ssem.at[layer],
-                gate_rsem.at[layer],
-                me_c,
-                peer,
-            ).start()
-        gate_recv[layer][me_h] = gate_send[layer][me_h]
+            cross_copy(0, head_peer(dx, dc)).start()
+        gate_recv[0][me_h] = out_send[0, me_h]
+
+    def cross_copy(layer, peer):
+        return remote(
+            out_send.at[layer, peer],
+            (gate_recv[0] if layer == 0 else q_buf[1]).at[me_h],
+            cross_ssem.at[layer],
+            cross_rsem.at[layer],
+            me_c,
+            peer,
+        )
+
+    def project_rows():
+        rows_all[0] = normed_rows()
+        scale = reciprocal(me_h // (HEADS // USERS))
+
+        def one(head):
+            gate, value, query, key = activations(rows_all[0], w_next[head])
+            gate_recv[1][head] = gate
+            own_buf[head] = own_term(query, key, value) * scale
+            return query
+
+        def body(step, carry):
+            head = lax.rem(me_h + step, HEADS)
+            out_send[1, head] = one(head)
+            cross_copy(1, head).start()
+            return carry
+
+        lax.fori_loop(1, HEADS, body, 0)
+        q_buf[1][me_h] = one(me_h)
 
     def att_copy(layer, peer):
         return remote(
@@ -315,35 +280,30 @@
 
     def attend(layer, user):
         per_user = HEADS // USERS
-        acc[...] = jnp.zeros_like(acc)
-
-        def body(i, carry):
-            first, second = [
-                arr[layer][jnp.clip(src[user * PAGES + 2 * i + k, 0], 0, ZERO)] for k in (0, 1)
-            ]
-            keys = jnp.concatenate([first[:, :DH], second[:, :DH]], axis=0)
-            values = jnp.concatenate([first[:, DH:], second[:, DH:]], axis=0)
-            for r in range(per_user):
-                score = lax.dot_general(
-                    q_buf[user * per_user + r],
-                    keys,
-                    (((1,), (1,)), ((), ())),
-                    preferred_element_type=F32,
-                )
-                weights = half_silu(score * (0.5 * DH**-0.5)).astype(BF16)
-                acc[r] += jnp.dot(weights, values, preferred_element_type=F32)
-            return carry
-
-        lax.fori_loop(0, PAGES // 2, body, 0)
-        scale = 1.0 / jnp.full((1, DH), lengths[user] * PAGE + 1, jnp.int32).astype(F32)
+        for p in range(PAGES):
+            page = arr[layer][jnp.clip(src[user * PAGES + p, 0], 0, ZERO)]
+            keys[pl.ds(p * PAGE, PAGE)] = page[:, :DH]
+            values[pl.ds(p * PAGE, PAGE)] = page[:, DH:]
+        query = q_buf[layer][pl.ds(user * per_user, per_user)].reshape(per_user * BLOCK, DH)
+        total = jnp.zeros((per_user * BLOCK, DH), F32)
+        for e in range(0, PAGES * PAGE, 2 * PAGE):
+            score = lax.dot_general(
+                query,
+                keys[pl.ds(e, 2 * PAGE)],
+                (((1,), (1,)), ((), ())),
+                preferred_element_type=F32,
+            )
+            weights = half_silu(score * (0.5 * DH**-0.5)).astype(BF16)
+            total = total + jnp.dot(
+                weights, values[pl.ds(e, 2 * PAGE)], preferred_element_type=F32
+            )
+        scale = reciprocal(user)
         for r in range(per_user):
             block = user * per_user + r
-            own = jnp.sum(
-                q_buf[block].astype(F32) * k_buf[block].astype(F32), axis=-1, keepdims=True
-            )
-            own = half_silu(own * (0.5 * DH**-0.5))
-            total = (acc[r] + own * v_buf[block].astype(F32)) * scale
-            att_send[layer][block] = total.astype(BF16)
+            here = total[r * BLOCK : (r + 1) * BLOCK]
+            if layer == 0:
+                here = here + own_term(q_buf[0][block], k_buf[block], v_buf[block])
+            att_send[layer][block] = (here * scale).astype(BF16)
         for r in range(per_user):
             block = user * per_user + r
 
@@ -356,9 +316,10 @@
                 att_recv[layer][block] = att_send[layer][block]
 
     def finish(layer):
-        wait_bytes(gate_recv[layer].at[pl.ds(0, HEADS - 1)], gate_rsem.at[layer])
         wait_bytes(att_recv[layer].at[pl.ds(0, HEADS - 1)], att_rsem.at[layer])
         att = [att_recv[layer][h].astype(F32) for h in range(HEADS)]
+        if layer == 1:
+            att = [att[h] + own_buf[h] for h in range(HEADS)]
         first = sum([jnp.sum(a, axis=-1, keepdims=True) for a in att]) * (1.0 / D)
         second = sum([jnp.sum(a * a, axis=-1, keepdims=True) for a in att]) * (1.0 / D)
         rstd = lax.rsqrt(second - first * first + 1e-05)
@@ -374,14 +335,6 @@
             )
         return update
 
-    def drain(layer):
-        wait_bytes(gate_send[layer].at[pl.ds(0, HEADS - 1)], gate_ssem.at[layer])
-        wait_bytes(att_send[layer].at[pl.ds(0, HEADS - 1)], att_ssem.at[layer])
-        wait_bytes(arr[layer].at[pl.ds(0, NZ * (NY - 1) * 2)], y_ssem.at[layer])
-        wait_bytes(pack[layer], z_ssem.at[layer])
-        rows_drain(layer)
-        w_drain(layer)
-
     def make_requests():
         count = USERS * PAGES
         lane = lax.broadcasted_iota(jnp.int32, (count, count), 1)
@@ -417,7 +370,7 @@
             req_out[z] = line
 
     state[...] = cand[...].astype(F32)
-    norm_rows(0)
+    rows_all[me_h] = normed_rows()
     make_requests()
     for layer in range(LAYERS):
         arr[layer][ZERO] = jnp.zeros((PAGE, 2 * DH), BF16)
@@ -437,7 +390,7 @@
     req_in[my_z] = req_out[my_z]
     for n in range(1, WINDOW):
         y_start(n)
-    rows_start(0)
+    spread_start(0, rows_all.at[me_h], rows_all)
     src_copy = pltpu.make_async_copy(src_vmem, src, smem_sem.at[1])
     src_copy.start()
     wait_bytes(req_in.at[pl.ds(0, NZ - 1)], req_rsem)
@@ -459,32 +412,34 @@
 
     for n in range(6):
         pack_send(n)
-    rows_wait(0)
-    project(0)
-    gate_start(0)
-    w_start()
+    spread_forward(0, rows_all)
+    spread_start(1, w_out.at[0], w_all[0])
+    spread_start(2, w_in.at[1], w_next)
+    w_all[0][me_h] = w_out[0]
+    w_all[1][me_h] = w_out[1]
+    w_next[me_h] = w_in[1]
+    spread_wait(0, rows_all)
+    project_head()
     for n in range(6, 11):
         pack_send(n)
-    for layer in range(LAYERS):
-        w_forward(layer)
+    spread_forward(1, w_all[0])
     pack_send(11)
     z_wait(0)
     attend(0, 0)
     attend(0, 1)
     pack_send(12)
-    for layer in range(LAYERS):
-        w_wait(layer)
-    update = finish(0)
-    state[...] = update.astype(BF16).astype(F32)
-    norm_rows(1)
-    rows_start(1)
-    for n in range(13, 15):
-        pack_send(n)
-    rows_wait(1)
-    project(1)
-    gate_start(1)
+    pack_send(13)
+    spread_drain(0, rows_all)
+    spread_forward(2, w_next)
+    spread_start(3, w_out.at[1], w_all[1])
+    spread_wait(1, w_all[0])
+    wait_bytes(gate_recv[0].at[pl.ds(0, HEADS - 1)], cross_rsem.at[0])
+    state[...] = finish(0).astype(BF16).astype(F32)
+    pack_send(14)
+    spread_wait(2, w_next)
+    project_rows()
     pack_send(15)
-    drain(0)
+    spread_forward(3, w_all[1])
     wait_bytes(req_in.at[pl.ds(0, NZ - 1)], req_ssem)
     wait_bytes(flag_in.at[pl.ds(0, NY - 1)], flag_rsem)
     wait_bytes(flag_in.at[pl.ds(0, NY - 1)], flag_ssem)
@@ -493,11 +448,22 @@
     to_smem.start()
     to_smem.wait()
     overflow[0] = flag_smem[0, 127]
+    wait_bytes(q_buf[1].at[pl.ds(0, HEADS - 1)], cross_rsem.at[1])
+    spread_wait(3, w_all[1])
+    spread_drain(1, w_all[0])
+    spread_drain(2, w_next)
+    spread_drain(3, w_all[1])
+    for layer in range(LAYERS):
+        wait_bytes(out_send.at[layer, pl.ds(0, HEADS - 1)], cross_ssem.at[layer])
+        wait_bytes(arr[layer].at[pl.ds(0, NZ * (NY - 1) * 2)], y_ssem.at[layer])
+    wait_bytes(pack[0], z_ssem.at[0])
+    wait_bytes(att_send[0].at[pl.ds(0, HEADS - 1)], att_ssem.at[0])
     z_wait(1)
     attend(1, 0)
     attend(1, 1)
     out[...] = finish(1).astype(BF16)
-    drain(1)
+    wait_bytes(pack[1], z_ssem.at[1])
+    wait_bytes(att_send[1].at[pl.ds(0, HEADS - 1)], att_ssem.at[1])
 
 
 def both(shape, dtype=BF16):
@@ -527,17 +493,20 @@
         scratch_shapes=[
             *both((NZ * C + 1, PAGE, 2 * DH)),
             *both((NZ - 1, C, PAGE, 2 * DH)),
-            *both((HEADS, BLOCK, D)),
             *both((HEADS, DH, D)),
             *both((HEADS, BLOCK, DH)),
             *both((HEADS, BLOCK, DH)),
             *both((HEADS, BLOCK, DH)),
             *both((HEADS, BLOCK, DH)),
             *[pltpu.VMEM((2 * NY, PAGE, 2 * DH), BF16)] * (LAYERS * NZ),
+            pltpu.VMEM((HEADS, BLOCK, D), BF16),
+            pltpu.VMEM((HEADS, D, 4 * DH), BF16),
             pltpu.VMEM((HEADS, BLOCK, DH), BF16),
             pltpu.VMEM((HEADS, BLOCK, DH), BF16),
-            pltpu.VMEM((HEADS, BLOCK, DH), BF16),
-            pltpu.VMEM((HEADS // USERS, BLOCK, DH), F32),
+            pltpu.VMEM((HEADS, BLOCK, DH), F32),
+            pltpu.VMEM((LAYERS, HEADS, BLOCK, DH), BF16),
+            pltpu.VMEM((PAGES * PAGE, DH), BF16),
+            pltpu.VMEM((PAGES * PAGE, DH), BF16),
             pltpu.VMEM((BLOCK, D), F32),
             pltpu.VMEM((NZ, 1, 128), jnp.int32),
             pltpu.VMEM((NZ, 1, 128), jnp.int32),
@@ -557,12 +526,8 @@
             dma,
             dma,
             dma((2,)),
-            dma((LAYERS, NX)),
-            dma((LAYERS, NX)),
-            dma((LAYERS, HEADS)),
-            dma((LAYERS, NX)),
-            dma((LAYERS, NX)),
-            dma((LAYERS, HEADS)),
+            dma((4,)),
+            dma((4, HEADS)),
             dma((LAYERS,)),
             dma((LAYERS,)),
             dma((LAYERS,)),

time: 186 us -> 175 us (0.941); the launches traced: 183 us -> 174 us
  Pallas kernels: 181 us -> 173 us
    pallas_call x1, Pallas kernels: 181 us -> 173 us  [run(): pl.pallas_call(functools.partial(kernel, C), out_shape=(jax.ShapeDtypeStr...]
where the time goes in v3:
time: 175 us; the launch traced here: 174 us
  Pallas kernels  173 us (99%)
    pallas_call x1, Pallas kernels, run(): pl.pallas_call(functools.partial(kernel, C), out_shape=(jax.ShapeDtypeStr...  173 us

profile of v3, /device:TPU:7, one launch (start us, length us, event | category | flops | bytes accessed | tf_op | source)
XLA Modules:
  0.0 174.5 jit_solution(12905924239346106914)
XLA Ops:
  0.0 0.0 copy-start.3
  0.0 0.0 copy-start.2
  0.0 0.0 copy-start.1
  0.0 0.0 copy-start
  0.0 172.8 %shard_map.66 = (bf16[256,1024]{1,0:T(8,128)(2,1)S(1)}, s32[1]{0:T(128)}) custom-call(s32[2]{0:T(128)} %lengths.1, s32[2,1,16]{2,1,0:T(1,128)} %bitcast.8, bf16[256,1024]{1,0:T(8,128)(2,1)} %cand.1, bf16[2,1024,512]{2,1,0:T(8,128)(2,1)} %w_in.1, bf16[2,128,1024]{2,1,0:T(8,128)(2,1)} %w_out.1, bf16[32,2,2,128,256]{4,3,2,1,0:T(8,128)(2,1)} %bitcast.6), custom_call_target="tpu_custom_call" | custom-call | tf_op jit(solution)/shard_map/pallas_call | solution.py:478
  173.4 0.0 copy-done.3
  173.4 0.0 copy-done.2
  173.4 0.0 copy-done.1
  173.4 0.0 copy-done
  173.4 0.3 conditional.1
  173.7 0.8 copy.14
Async XLA Ops:
  0.0 173.4 %copy-start.3 = (s32[2]{0:T(128)S(1)}, s32[2]{0:T(128)}, u32[]{:S(2)}) copy-start(s32[2]{0:T(128)} %lengths.1) | copy-start | bytes 28
  0.0 173.4 %copy-start.2 = (s32[2,16,1]{1,2,0:T(1,128)S(1)}, s32[2,16,1]{1,2,0:T(1,128)}, u32[]{:S(2)}) copy-start(s32[2,16,1]{1,2,0:T(1,128)} %param.12) | copy-start | bytes 388
  0.0 173.4 %copy-start.1 = (bf16[2,128,1024]{2,1,0:T(8,128)(2,1)S(1)}, bf16[2,128,1024]{2,1,0:T(8,128)(2,1)}, u32[]{:S(2)}) copy-start(bf16[2,128,1024]{2,1,0:T(8,128)(2,1)} %w_out.1) | copy-start | bytes 1572868
  0.0 173.4 %copy-start = (bf16[256,1024]{1,0:T(8,128)(2,1)S(1)}, bf16[256,1024]{1,0:T(8,128)(2,1)}, u32[]{:S(2)}) copy-start(bf16[256,1024]{1,0:T(8,128)(2,1)} %cand.1) | copy-start | bytes 1572868

commit v4 on v3

v4 whole, which is shorter than its diff:
```python
import functools

import jax
import jax.numpy as jnp
from jax import lax
from jax.experimental import pallas as pl
from jax.experimental.pallas import tpu as pltpu
from jax.sharding import PartitionSpec as P

MESH = pl.DeviceIdType.MESH
DH = 128
D = 1024
PAGE = 128
LAYERS = 2
USERS = 2
PAGES = 16
NY = 4
NZ = 8
NX = 4
HEADS = 8
BLOCK = 256
MOST = 2 * NY
CAPS = (5, 6, MOST)
WINDOW = 3
OFFSETS = (4, 3, 5, 2, 6, 1, 7, 0)
F32 = jnp.float32
BF16 = jnp.bfloat16


def half_silu(t):
    return t * jnp.tanh(t) + t


def remote(src_ref, dst_ref, send, recv, cache, head):
    return pltpu.make_async_remote_copy(
        src_ref=src_ref,
        dst_ref=dst_ref,
        send_sem=send,
        recv_sem=recv,
        device_id=(cache, head),
        device_id_type=MESH,
    )


def wait_bytes(ref, sem):
    pltpu.make_async_copy(ref, ref, sem).wait()


def place_of_device():
    me_c = lax.axis_index("cache")
    my_y = me_c // NZ
    my_z = lax.rem(me_c, NZ)

    def y_peer(dy):
        return lax.rem(my_y + dy, NY)

    def z_peer(dz):
        return lax.rem(my_z + dz, NZ)

    return me_c, lax.axis_index("head"), my_y, my_z, y_peer, z_peer


def greet(devices):
    barrier = pltpu.get_barrier_semaphore()
    for device in devices:
        pl.semaphore_signal(barrier, inc=1, device_id=device, device_id_type=MESH)
    return lambda: pl.semaphore_wait(barrier, len(devices))


def y_copies(pool, target, n, send, recv):
    me_c, me_h, my_y, my_z, y_peer, z_peer = place_of_device()
    layer, i = divmod(n, NZ)
    column = z_peer(OFFSETS[i])
    place = target.at[pl.ds(my_y * 2, 2)]
    for dy in (2, 1, 3):
        remote(
            pool.at[y_peer(dy) * NZ + column, :, layer],
            place,
            send,
            recv,
            y_peer(dy) * NZ + my_z,
            me_h,
        ).start()
    pltpu.make_async_copy(pool.at[my_y * NZ + column, :, layer], place, recv).start()


def request_kernel(
    lengths,
    owners,
    pool,
    src,
    req_in,
    y_first,
    level,
    req_out,
    flag_out,
    flag_in,
    flag_all,
    flag_smem,
    y_ssem,
    y_rsem,
    req_ssem,
    req_rsem,
    flag_ssem,
    flag_rsem,
    smem_sem,
):
    me_c, me_h, my_y, my_z, y_peer, z_peer = place_of_device()
    greeted = greet(
        [(y_peer(dy) * NZ + my_z, me_h) for dy in range(1, NY)]
        + [(my_y * NZ + z_peer(dz), me_h) for dz in range(1, NZ)]
    )
    count = USERS * PAGES
    lane = lax.broadcasted_iota(jnp.int32, (count, count), 1)
    sub = lax.broadcasted_iota(jnp.int32, (count, count), 0)
    row = jnp.zeros((1, count), jnp.int32)
    col = jnp.zeros((count, 1), jnp.int32)
    for p in range(count):
        owner = owners[p // PAGES, 0, p % PAGES]
        row = jnp.where(lane[:1] == p, owner, row)
        col = jnp.where(sub[:, :1] == p, owner, col)

    def live_of(index):
        length = jnp.where(index < PAGES, lengths[0], lengths[1])
        return lax.rem(index, PAGES) < length

    def total(mask, axis):
        return jnp.sum(mask.astype(jnp.int32), axis=axis, keepdims=True)

    slot = jnp.minimum(total((row == col) & (lane < sub), 1), 1)
    same = lax.rem(row, NZ) == lax.rem(col, NZ)
    rank = total(same & (lane < sub) & live_of(lane), 1)
    live = live_of(sub[:, :1])
    place = lax.rem(col // NZ, NY) * 2 + slot
    target = jnp.where(live, lax.rem(col, NZ) * MOST + rank, NZ * MOST)
    need = jnp.max(jnp.where(live, rank + 1, 0), axis=0, keepdims=True)
    rank_row = total(same & (sub < lane) & live_of(sub), 0)
    target_row = jnp.where(live_of(lane[:1]), lax.rem(row, NZ) * MOST + rank_row, NZ * MOST)
    src[...] = jnp.zeros_like(src)
    src[:, 0:count] = target_row
    lanes = lax.broadcasted_iota(jnp.int32, (count, 128), 1)
    for z in range(NZ):
        hit = (target == lanes + z * MOST) & (lanes < MOST)
        line = jnp.sum(jnp.where(hit, place, 0), axis=0, keepdims=True)
        req_out[z] = jnp.where(lanes[:1] == 127, need, line)

    greeted()
    for dz in range(1, NZ):
        column = z_peer(dz)
        remote(
            req_out.at[column],
            req_in.at[my_z],
            req_ssem,
            req_rsem,
            my_y * NZ + column,
            me_h,
        ).start()
    y_copies(pool, y_first, 0, y_ssem, y_rsem)
    req_in[my_z] = req_out[my_z]
    wait_bytes(req_out.at[pl.ds(0, NZ - 1)], req_rsem)
    flag_out[0] = jnp.max(req_in[...], axis=0)
    for dy in range(1, NY):
        remote(
            flag_out.at[0],
            flag_in.at[my_y],
            flag_ssem,
            flag_rsem,
            y_peer(dy) * NZ + my_z,
            me_h,
        ).start()
    flag_in[my_y] = flag_out[0]
    wait_bytes(req_out.at[pl.ds(0, NY - 1)], flag_rsem)
    most = jnp.max(flag_in[...], axis=0)
    flag_all[...] = (most > CAPS[0]).astype(jnp.int32) + (most > CAPS[1]).astype(jnp.int32)
    to_smem = pltpu.make_async_copy(flag_all, flag_smem, smem_sem)
    to_smem.start()
    to_smem.wait()
    level[0] = flag_smem[0, 127]
    wait_bytes(req_out.at[pl.ds(0, NZ - 1)], req_ssem)
    wait_bytes(req_out.at[pl.ds(0, NY - 1)], flag_ssem)
    wait_bytes(y_first.at[pl.ds(0, 2 * (NY - 1))], y_ssem)
    wait_bytes(y_first, y_rsem)


def kernel(
    C,
    lengths,
    src,
    req,
    cand,
    w_in,
    w_out,
    y_first,
    pool,
    out,
    *scratch,
):
    (
        arr,
        pack,
        w_all,
        gate_recv,
        q_buf,
        att_send,
        att_recv,
    ) = [scratch[2 * i : 2 * i + 2] for i in range(7)]
    ybuf = (y_first, *scratch[14:29])
    (
        rows_all,
        w_next,
        k_buf,
        v_buf,
        own_buf,
        out_send,
        keys,
        values,
        state,
        y_ssem,
        y_rsem,
        z_ssem,
        z_rsem,
        spread_ssem,
        spread_rsem,
        cross_ssem,
        cross_rsem,
        att_ssem,
        att_rsem,
    ) = scratch[29:]

    ZERO = NZ * C
    me_c, me_h, my_y, my_z, y_peer, z_peer = place_of_device()
    my_x = me_h // 2
    core = lax.rem(me_h, 2)
    sibling = my_x * 2 + (1 - core)

    def head_peer(dx, dcore):
        return lax.rem(my_x + dx, NX) * 2 + lax.rem(core + dcore, 2)

    head_steps = [(dx, dc) for dx in range(NX) for dc in range(2) if (dx, dc) != (0, 0)]
    greeted = greet(
        [(y_peer(dy) * NZ + my_z, me_h) for dy in range(1, NY)]
        + [(my_y * NZ + z_peer(dz), me_h) for dz in range(1, NZ)]
        + [(me_c, head_peer(dx, dc)) for dx, dc in head_steps]
    )

    def y_start(n):
        y_copies(pool, ybuf[n], n, y_ssem.at[n], y_rsem.at[n])

    def pack_send(n):
        if n + WINDOW < LAYERS * NZ:
            y_start(n + WINDOW)
        layer, i = divmod(n, NZ)
        if n > 0:
            wait_bytes(ybuf[n], y_rsem.at[n])
        column = z_peer(OFFSETS[i])
        for j in range(C):
            page = ybuf[n][jnp.clip(req[column, 0, j], 0, MOST - 1)]
            if OFFSETS[i] == 0:
                arr[layer][my_z * C + j] = page
            else:
                pack[layer][i, j] = page
        if OFFSETS[i] != 0:
            remote(
                pack[layer].at[i],
                arr[layer].at[pl.ds(my_z * C, C)],
                z_ssem.at[layer],
                z_rsem.at[layer],
                my_y * NZ + column,
                me_h,
            ).start()

    def z_wait(layer):
        wait_bytes(arr[layer].at[pl.ds(0, (NZ - 1) * C)], z_rsem.at[layer])

    def spread_start(k, block, places):
        for dx in (2, 1, 3):
            remote(
                block,
                places.at[me_h],
                spread_ssem.at[k],
                spread_rsem.at[k, me_h],
                me_c,
                head_peer(dx, 0),
            ).start()
        remote(
            block, places.at[me_h], spread_ssem.at[k], spread_rsem.at[k, me_h], me_c, sibling
        ).start()

    def spread_forward(k, places):
        for dx in (1, 3, 2):
            source = head_peer(dx, 0)
            place = places.at[source]
            wait_bytes(place, spread_rsem.at[k, source])
            remote(
                place, place, spread_ssem.at[k], spread_rsem.at[k, source], me_c, sibling
            ).start()

    def spread_wait(k, places):
        for dx in (0, 1, 3, 2):
            source = head_peer(dx, 1)
            wait_bytes(places.at[source], spread_rsem.at[k, source])

    def spread_drain(k, places):
        wait_bytes(places.at[pl.ds(0, HEADS - 1)], spread_ssem.at[k])

    def normed_rows():
        xf = state[...]
        normed = xf * lax.rsqrt(jnp.mean(xf * xf, axis=-1, keepdims=True) + 1e-06)
        return normed.astype(BF16)

    def activations(rows, w):
        act = jnp.dot(rows, w, preferred_element_type=F32)
        act = half_silu(act * 0.5).astype(BF16)
        return [act[:, i * DH : (i + 1) * DH] for i in range(4)]

    def reciprocal(user):
        return 1.0 / jnp.full((1, DH), lengths[user] * PAGE + 1, jnp.int32).astype(F32)

    def own_term(query, key, value):
        own = jnp.sum(query.astype(F32) * key.astype(F32), axis=-1, keepdims=True)
        return half_silu(own * (0.5 * DH**-0.5)) * value.astype(F32)

    def project_head():
        def body(i, carry):
            gate, value, query, key = activations(rows_all[i], w_in[0])
            out_send[0, i] = gate
            v_buf[i] = value
            q_buf[0][i] = query
            k_buf[i] = key
            return carry

        lax.fori_loop(0, HEADS, body, 0)
        for dx, dc in head_steps:
            cross_copy(0, head_peer(dx, dc)).start()
        gate_recv[0][me_h] = out_send[0, me_h]

    def cross_copy(layer, peer):
        return remote(
            out_send.at[layer, peer],
            (gate_recv[0] if layer == 0 else q_buf[1]).at[me_h],
            cross_ssem.at[layer],
            cross_rsem.at[layer],
            me_c,
            peer,
        )

    def project_rows():
        rows_all[0] = normed_rows()
        scale = reciprocal(me_h // (HEADS // USERS))

        def one(head):
            gate, value, query, key = activations(rows_all[0], w_next[head])
            gate_recv[1][head] = gate
            own_buf[head] = own_term(query, key, value) * scale
            return query

        def body(step, carry):
            head = lax.rem(me_h + step, HEADS)
            out_send[1, head] = one(head)
            cross_copy(1, head).start()
            return carry

        lax.fori_loop(1, HEADS, body, 0)
        q_buf[1][me_h] = one(me_h)

    def att_copy(layer, peer):
        return remote(
            att_send[layer].at[peer],
            att_recv[layer].at[me_h],
            att_ssem.at[layer],
            att_rsem.at[layer],
            me_c,
            peer,
        )

    def attend(layer):
        per_user = HEADS // USERS

        def body(user, carry):
            for p in range(PAGES):
                target = src[0, user * PAGES + p]
                page = arr[layer][
                    jnp.clip((target // MOST) * C + lax.rem(target, MOST), 0, ZERO)
                ]
                keys[pl.ds(p * PAGE, PAGE)] = page[:, :DH]
                values[pl.ds(p * PAGE, PAGE)] = page[:, DH:]
            query = q_buf[layer][pl.ds(user * per_user, per_user)]
            query = query.reshape(per_user * BLOCK, DH)
            total = jnp.zeros((per_user * BLOCK, DH), F32)
            for e in range(0, PAGES * PAGE, 2 * PAGE):
                score = lax.dot_general(
                    query,
                    keys[pl.ds(e, 2 * PAGE)],
                    (((1,), (1,)), ((), ())),
                    preferred_element_type=F32,
                )
                weights = half_silu(score * (0.5 * DH**-0.5)).astype(BF16)
                total = total + jnp.dot(
                    weights, values[pl.ds(e, 2 * PAGE)], preferred_element_type=F32
                )
            scale = reciprocal(user)
            for r in range(per_user):
                block = user * per_user + r
                here = total[r * BLOCK : (r + 1) * BLOCK]
                if layer == 0:
                    here = here + own_term(q_buf[0][block], k_buf[block], v_buf[block])
                att_send[layer][block] = (here * scale).astype(BF16)
            for r in range(per_user):
                block = user * per_user + r

                @pl.when(block != me_h)
                def _():
                    att_copy(layer, block).start()

                @pl.when(block == me_h)
                def _():
                    att_recv[layer][block] = att_send[layer][block]

            return carry

        lax.fori_loop(0, USERS, body, 0)

    def finish(layer):
        wait_bytes(att_recv[layer].at[pl.ds(0, HEADS - 1)], att_rsem.at[layer])
        att = [att_recv[layer][h].astype(F32) for h in range(HEADS)]
        if layer == 1:
            att = [att[h] + own_buf[h] for h in range(HEADS)]
        first = sum([jnp.sum(a, axis=-1, keepdims=True) for a in att]) * (1.0 / D)
        second = sum([jnp.sum(a * a, axis=-1, keepdims=True) for a in att]) * (1.0 / D)
        rstd = lax.rsqrt(second - first * first + 1e-05)
        update = state[...]
        for h in range(0, HEADS, 2):
            pair = [
                ((att[i] - first) * rstd * gate_recv[layer][i].astype(F32)).astype(BF16)
                for i in (h, h + 1)
            ]
            w_pair = jnp.concatenate([w_all[layer][h], w_all[layer][h + 1]], axis=0)
            update = update + jnp.dot(
                jnp.concatenate(pair, axis=1), w_pair, preferred_element_type=F32
            )
        return update

    state[...] = cand[...].astype(F32)
    rows_all[me_h] = normed_rows()
    for layer in range(LAYERS):
        arr[layer][ZERO] = jnp.zeros((PAGE, 2 * DH), BF16)
    greeted()
    for n in range(1, WINDOW):
        y_start(n)
    pack_send(0)
    spread_start(0, rows_all.at[me_h], rows_all)
    for n in range(1, 6):
        pack_send(n)
    spread_forward(0, rows_all)
    spread_start(1, w_out.at[0], w_all[0])
    spread_start(2, w_in.at[1], w_next)
    w_all[0][me_h] = w_out[0]
    w_all[1][me_h] = w_out[1]
    w_next[me_h] = w_in[1]
    spread_wait(0, rows_all)
    project_head()
    for n in range(6, 11):
        pack_send(n)
    spread_forward(1, w_all[0])
    pack_send(11)
    z_wait(0)
    attend(0)
    pack_send(12)
    pack_send(13)
    spread_drain(0, rows_all)
    spread_forward(2, w_next)
    spread_start(3, w_out.at[1], w_all[1])
    spread_wait(1, w_all[0])
    wait_bytes(gate_recv[0].at[pl.ds(0, HEADS - 1)], cross_rsem.at[0])
    state[...] = finish(0).astype(BF16).astype(F32)
    pack_send(14)
    spread_wait(2, w_next)
    project_rows()
    pack_send(15)
    spread_forward(3, w_all[1])
    wait_bytes(q_buf[1].at[pl.ds(0, HEADS - 1)], cross_rsem.at[1])
    spread_wait(3, w_all[1])
    spread_drain(1, w_all[0])
    spread_drain(2, w_next)
    spread_drain(3, w_all[1])
    for layer in range(LAYERS):
        wait_bytes(out_send.at[layer, pl.ds(0, HEADS - 1)], cross_ssem.at[layer])
    for n in range(1, LAYERS * NZ):
        wait_bytes(ybuf[n].at[pl.ds(0, 2 * (NY - 1))], y_ssem.at[n])
    wait_bytes(pack[0], z_ssem.at[0])
    wait_bytes(att_send[0].at[pl.ds(0, HEADS - 1)], att_ssem.at[0])
    z_wait(1)
    attend(1)
    out[...] = finish(1).astype(BF16)
    wait_bytes(pack[1], z_ssem.at[1])
    wait_bytes(att_send[1].at[pl.ds(0, HEADS - 1)], att_ssem.at[1])


def both(shape, dtype=BF16):
    return [pltpu.VMEM(shape, dtype)] * LAYERS


def ask(lengths, owners, pool):
    dma = pltpu.SemaphoreType.DMA
    vmem = pl.BlockSpec(memory_space=pltpu.VMEM)
    smem = pl.BlockSpec(memory_space=pltpu.SMEM)
    return pl.pallas_call(
        request_kernel,
        out_shape=(
            jax.ShapeDtypeStruct((1, 128), jnp.int32),
            jax.ShapeDtypeStruct((NZ, 1, 128), jnp.int32),
            jax.ShapeDtypeStruct((2 * NY, PAGE, 2 * DH), BF16),
            jax.ShapeDtypeStruct((1,), jnp.int32),
        ),
        in_specs=[smem, smem, pl.BlockSpec(memory_space=pl.ANY)],
        out_specs=(vmem, vmem, vmem, smem),
        scratch_shapes=[
            pltpu.VMEM((NZ, 1, 128), jnp.int32),
            pltpu.VMEM((1, 1, 128), jnp.int32),
            pltpu.VMEM((NY, 1, 128), jnp.int32),
            pltpu.VMEM((1, 128), jnp.int32),
            pltpu.SMEM((1, 128), jnp.int32),
            *[dma] * 7,
        ],
        compiler_params=pltpu.CompilerParams(collective_id=0, has_side_effects=True),
    )(lengths, owners, pool)


def run(turn, *args):
    C = CAPS[turn]
    dma = pltpu.SemaphoreType.DMA
    vmem = pl.BlockSpec(memory_space=pltpu.VMEM)
    smem = pl.BlockSpec(memory_space=pltpu.SMEM)
    return pl.pallas_call(
        functools.partial(kernel, C),
        out_shape=jax.ShapeDtypeStruct((BLOCK, D), BF16),
        in_specs=[
            smem,
            smem,
            smem,
            vmem,
            vmem,
            vmem,
            vmem,
            pl.BlockSpec(memory_space=pl.ANY),
        ],
        out_specs=vmem,
        scratch_shapes=[
            *both((NZ * C + 1, PAGE, 2 * DH)),
            *both((NZ - 1, C, PAGE, 2 * DH)),
            *both((HEADS, DH, D)),
            *both((HEADS, BLOCK, DH)),
            *both((HEADS, BLOCK, DH)),
            *both((HEADS, BLOCK, DH)),
            *both((HEADS, BLOCK, DH)),
            *[pltpu.VMEM((2 * NY, PAGE, 2 * DH), BF16)] * (LAYERS * NZ - 1),
            pltpu.VMEM((HEADS, BLOCK, D), BF16),
            pltpu.VMEM((HEADS, D, 4 * DH), BF16),
            pltpu.VMEM((HEADS, BLOCK, DH), BF16),
            pltpu.VMEM((HEADS, BLOCK, DH), BF16),
            pltpu.VMEM((HEADS, BLOCK, DH), F32),
            pltpu.VMEM((LAYERS, HEADS, BLOCK, DH), BF16),
            pltpu.VMEM((PAGES * PAGE, DH), BF16),
            pltpu.VMEM((PAGES * PAGE, DH), BF16),
            pltpu.VMEM((BLOCK, D), F32),
            dma((LAYERS * NZ,)),
            dma((LAYERS * NZ,)),
            dma((LAYERS,)),
            dma((LAYERS,)),
            dma((4,)),
            dma((4, HEADS)),
            dma((LAYERS,)),
            dma((LAYERS,)),
            dma((LAYERS,)),
            dma((LAYERS,)),
        ],
        compiler_params=pltpu.CompilerParams(
            collective_id=turn + 1, has_side_effects=True, vmem_limit_bytes=62 * 2**20
        ),
    )(*args)


def shards(candidates, proj_in, proj_out, page_pool, page_owner, history_pages):
    pool = page_pool[0]
    src, req, y_first, level = ask(history_pages, page_owner.transpose(0, 2, 1), pool)
    args = (history_pages, src, req, candidates, proj_in, proj_out, y_first, pool)
    return lax.switch(level[0], [functools.partial(run, turn, *args) for turn in range(len(CAPS))])


def solution(mesh):
    return jax.shard_map(
        shards,
        mesh=mesh,
        in_specs=(
            P(("cache", "head"), None),
            P(None, None, "head"),
            P(None, "head", None),
            P("cache", None, None, None, None, "head"),
            P("cache", None, None),
            P("cache"),
        ),
        out_specs=P(("cache", "head"), None),
        check_vma=False,
    )
```

time: 175 us -> 181 us (1.034)
  Pallas kernels: 173 us -> 177 us
    pallas_call x1 -> x2, Pallas kernels: 173 us -> 177 us  [the longest x1 158 us: run(): pl.pallas_call(functools.partial(kernel, C), out_shape=jax.ShapeDtypeStru...]
where the time goes in v4:
time: 181 us; the launch traced here: 180 us
  Pallas kernels  177 us (98%)
  local copies, waits for them, and re-layouts  1.88 us (1%)
    pallas_call x1, Pallas kernels, run(): pl.pallas_call(functools.partial(kernel, C), out_shape=jax.ShapeDtypeStru...  158 us
    pallas_call x1, Pallas kernels, ask(): pl.pallas_call(request_kernel, out_shape=(jax.ShapeDtypeStruct((1, 128),...  18.6 us

profile of v4, /device:TPU:7, one launch (start us, length us, event | category | flops | bytes accessed | tf_op | source)
XLA Modules:
  0.0 180.3 jit_solution(10602729441886577507)
XLA Ops:
  0.0 0.0 copy-start.2
  0.0 0.0 copy-start.1
  0.0 0.0 copy-start
  0.0 18.6 %shard_map.67 = (s32[1,128]{1,0:T(1,128)S(1)}, s32[8,1,128]{2,1,0:T(1,128)S(1)}, bf16[8,128,256]{2,1,0:T(8,128)(2,1)S(1)}, s32[1]{0:T(128)}) custom-call(s32[2]{0:T(128)} %lengths.1, s32[2,1,16]{2,1,0:T(1,128)} %bitcast.9, bf16[32,2,2,128,256]{4,3,2,1,0:T(8,128)(2,1)} %bitcast.5), custom_call_target="tpu_custom_call" | custom-call | tf_op jit(solution)/shard_map/pallas_call | solution.py:507
  19.2 0.0 copy-done.2
  19.2 0.0 copy-done.1
  19.2 0.0 copy-done
  19.2 159.2 %conditional.1 = (bf16[256,1024]{1,0:T(8,128)(2,1)}) conditional(s32[]{:T(128)} %bitcast.3, (s32[2]{0:T(128)S(1)}, s32[1,128]{1,0:T(1,128)S(1)}, s32[8,1,128]{2,1,0:T(1,128)S(1)}, bf16[256,1024]{1,0:T(8,128)(2,1)S(1)}, bf16[2,1024,512]{2,1,0:T(8,128)(2,1)}, /*index=5*/bf16[2,128,1024]{2,1,0:T(8,128)(2,1)S(1)}, ...), branch_computations={%region_0.0_spmd, %region_1.0_spmd, %region_2.0_spmd} | conditional | bytes 8 | solution.py:587
  19.5 158.5 %branch_1_fun.1 = bf16[256,1024]{1,0:T(8,128)(2,1)} custom-call(s32[2]{0:T(128)S(1)} %get-tuple-element.65.lengths, s32[1,128]{1,0:T(1,128)S(1)} %get-tuple-element.66.src, s32[8,1,128]{2,1,0:T(1,128)S(1)} %get-tuple-element.67.req, bf16[256,1024]{1,0:T(8,128)(2,1)S(1)} %get-tuple-element.68.cand, bf16[2,1024,512]{2,1,0:T(8,128)(2,1)} %get-tuple-element.69.w_in, ...), custom_call_target="tpu_custom_call" | custom-call | tf_op jit(solution)/shard_map/cond/branch_1_fun/pallas_call | solution.py:534
  178.5 1.9 %copy.15 = bf16[256,1024]{1,0:T(8,128)(2,1)} copy(bf16[256,1024]{1,0:T(8,128)(2,1)} %get-tuple-element.89) | data formatting | bytes 1048576
Async XLA Ops:
  0.0 19.2 %copy-start.2 = (s32[2]{0:T(128)S(1)}, s32[2]{0:T(128)}, u32[]{:S(2)}) copy-start(s32[2]{0:T(128)} %lengths.1) | copy-start | bytes 28
  0.0 19.2 %copy-start.1 = (bf16[2,128,1024]{2,1,0:T(8,128)(2,1)S(1)}, bf16[2,128,1024]{2,1,0:T(8,128)(2,1)}, u32[]{:S(2)}) copy-start(bf16[2,128,1024]{2,1,0:T(8,128)(2,1)} %param.11) | copy-start | bytes 1572868
  0.0 19.2 %copy-start = (bf16[256,1024]{1,0:T(8,128)(2,1)S(1)}, bf16[256,1024]{1,0:T(8,128)(2,1)}, u32[]{:S(2)}) copy-start(bf16[256,1024]{1,0:T(8,128)(2,1)} %param.9) | copy-start | bytes 1572868
